TPU v7x, 32 devices: a whole 2x2x4 slice. The times are simulated.
32 devices in a mesh: gx: 4 (over x, core), gy: 2 (over y), obs: 4 (over z).
Axes of the slice: x: 2, y: 2, z: 4, core: 2. Of those that a mesh axis runs over, the one named last changes fastest.
Arguments:
- control: float32 [4, 4, 256, 512], P(None, 'obs', 'gy', 'gx'), may hold values from -6 to 6
- diffusivity: float32 [2, 4, 256, 512], P(None, 'obs', 'gy', 'gx'), may hold values from 0.12 to 0.245
- prof_tile: int32 [4096, 1], P(('gx', 'gy')), may hold values from 0 to 7; in each aligned block of 512 rows (0 to 511, 512 to 1023, ...) at most 128 rows name the same one
- prof_cell: int32 [4096], P(('gx', 'gy')), may hold values from 0 to 16383
- obs_prof: int32 [16384], P(('gx', 'gy', 'obs')), may hold values from 0 to 511
- obs_field: int32 [16384], P(('gx', 'gy', 'obs')), may hold values from 0 to 3
- obs_level: int32 [16384], P(('gx', 'gy', 'obs')), may hold values from 0 to 2
- obs_weight: float32 [16384], P(('gx', 'gy', 'obs')), may hold values from 0 to 1
- innovation: float32 [16384], P(('gx', 'gy', 'obs')), may hold values from -6 to 6
- obs_precision: float32 [16384], P(('gx', 'gy', 'obs')), may hold values from 0.25 to 4
Outputs:
- gradient: float32 [4, 4, 256, 512], P(None, 'obs', 'gy', 'gx')
- departures: float32 [16384], P(('gx', 'gy', 'obs'))
Inputs may be any that keep to these rules, and one draw needn't show every extreme that they name: `prof_tile`: in each aligned block of 512 rows (the profiles of one tile) no tile is named by more than 128 rows; in some blocks one tile is named by exactly 128 rows.
All inputs are finite; a program needn't handle non-finite values.
Results may differ from a plain program's by a relative error of at most 0.00002.
Values sent between devices are 32-bit elements; how exact they have to be, the bound alone decides.
A program may use at most 64 MiB of HBM per device.

v0:
```python
import jax
import jax.numpy as jnp
from jax import lax
from jax.sharding import PartitionSpec as P

STEPS = 10


def passed_along(value, axis, by):
    length = lax.axis_size(axis)
    return lax.ppermute(value, axis, [(i, (i + by) % length) for i in range(length)])


def shifted(block, axis, distance):
    devices = range(lax.axis_size(axis))
    route = [(i - distance, i) for i in devices if i - distance in devices]
    return lax.ppermute(block, axis, route)


def with_halo(block, sides, width):
    for axis, dim in sides:
        count = lax.axis_size(axis)
        forward = [(i, i + 1) for i in range(count - 1)]
        forward.append((count - 1, 0))
        backward = [(target, source) for source, target in forward]
        low = lax.ppermute(
            lax.slice_in_dim(block, block.shape[dim] - width, None, axis=dim), axis, forward
        )
        high = lax.ppermute(lax.slice_in_dim(block, 0, width, axis=dim), axis, backward)
        block = jnp.concatenate([low, block, high], axis=dim)
    return block


def advance(padded, east_rate, north_rate):
    center = padded[:, :, 1:-1, 1:-1]
    east_flux = east_rate[:, 1:-1, 1:-1] * (padded[:, :, 1:-1, 2:] - center)
    west_flux = east_rate[:, 1:-1, :-2] * (padded[:, :, 1:-1, :-2] - center)
    north_flux = north_rate[:, 1:-1, 1:-1] * (padded[:, :, 2:, 1:-1] - center)
    south_flux = north_rate[:, :-2, 1:-1] * (padded[:, :, :-2, 1:-1] - center)
    return center + east_flux + west_flux + north_flux + south_flux


def per_device(
    control,
    diffusivity,
    prof_tile,
    prof_cell,
    obs_prof,
    obs_field,
    obs_level,
    obs_weight,
    innovation,
    obs_precision,
):
    level_count = control.shape[1]
    lat_cells = control.shape[2]
    lon_cells = control.shape[3]
    field_count = control.shape[0]
    flat_levels = field_count * level_count
    grid_gx = lax.axis_size("gx")
    grid_gy = lax.axis_size("gy")
    holders = grid_gx * grid_gy
    prof_count = prof_tile.shape[0]
    capacity = max(2, 2 * prof_count // holders)
    all_levels = level_count * lax.axis_size("obs")
    row_index = lax.axis_index("gy") * lat_cells + jnp.arange(lat_cells, dtype=jnp.int32)
    north_mask = (row_index != grid_gy * lat_cells - 1).astype(jnp.float32)
    east_own = diffusivity[0]
    north_own = diffusivity[1] * north_mask[None, :, None]
    west_column = passed_along(east_own[:, :, -1:], "gx", 1)
    south_row = shifted(north_own[:, -1:, :], "gy", 1)
    east_wide = jnp.concatenate([west_column, east_own, jnp.zeros_like(west_column)], axis=2)
    east_padded = jnp.pad(east_wide, ((0, 0), (1, 1), (0, 0)))
    north_tall = jnp.concatenate([south_row, north_own, jnp.zeros_like(south_row)], axis=1)
    north_padded = jnp.pad(north_tall, ((0, 0), (0, 0), (1, 1)))

    def diffuse(field):

        def sweep(step_index, values):
            rimmed = with_halo(values, (("gx", 3), ("gy", 2)), 1)
            return advance(rimmed, east_padded, north_padded)

        return lax.fori_loop(0, STEPS, sweep, field)

    increment = diffuse(control)
    flat_field = increment.reshape(flat_levels, lat_cells * lon_cells)
    holder_of = prof_tile[:, 0]
    one_hot = (holder_of[:, None] == jnp.arange(holders, dtype=jnp.int32)[None, :]).astype(
        jnp.int32
    )
    earlier = jnp.cumsum(one_hot, axis=0) - one_hot
    slot_of = jnp.sum(earlier * one_hot, axis=1)
    position = holder_of * capacity + slot_of
    requests = jnp.zeros((holders * capacity,), jnp.int32).at[position].set(prof_cell)
    asked = lax.all_to_all(
        requests.reshape(holders, 1, capacity),
        ("gx", "gy"),
        split_axis=0,
        concat_axis=0,
        tiled=True,
    )
    found = jnp.take(flat_field, asked[:, 0, :], axis=1)
    found = jnp.transpose(found, (1, 0, 2))
    returned = lax.all_to_all(found, ("gx", "gy"), split_axis=0, concat_axis=0, tiled=True)
    slab = jnp.transpose(returned, (1, 0, 2)).reshape(flat_levels, holders * capacity)[:, position]
    slab = slab.reshape(field_count, level_count, prof_count)
    columns = lax.all_gather(slab, "obs", axis=1, tiled=True)
    flat_columns = columns.reshape(-1)
    lower_index = (obs_field * all_levels + obs_level) * prof_count + obs_prof
    upper_index = lower_index + prof_count
    observed = (
        obs_weight * flat_columns[lower_index] + (1.0 - obs_weight) * flat_columns[upper_index]
    )
    departures = obs_precision * (observed - innovation)
    lower_share = obs_weight * departures
    upper_share = (1.0 - obs_weight) * departures
    adjoint_full = jnp.zeros((field_count * all_levels * prof_count,), jnp.float32)
    adjoint_full = adjoint_full.at[lower_index].add(lower_share).at[upper_index].add(upper_share)
    adjoint_full = adjoint_full.reshape(field_count, all_levels, prof_count)
    adjoint_slab = lax.psum_scatter(adjoint_full, "obs", scatter_dimension=1, tiled=True)
    adjoint_slab = adjoint_slab.reshape(flat_levels, prof_count)
    outgoing = (
        jnp.zeros((holders * capacity, flat_levels), jnp.float32).at[position].set(adjoint_slab.T)
    )
    outgoing = jnp.transpose(outgoing.reshape(holders, capacity, flat_levels), (0, 2, 1))
    incoming = lax.all_to_all(outgoing, ("gx", "gy"), split_axis=0, concat_axis=0, tiled=True)
    cells = asked.reshape(holders * capacity)
    amounts = jnp.transpose(incoming, (1, 0, 2)).reshape(flat_levels, holders * capacity)
    pulled = jnp.zeros((flat_levels, lat_cells * lon_cells), jnp.float32).at[:, cells].add(amounts)
    pulled = pulled.reshape(field_count, level_count, lat_cells, lon_cells)
    gradient = control + diffuse(pulled)
    return (gradient, departures)


def solution(mesh):
    in_specs = (
        P(None, "obs", "gy", "gx"),
        P(None, "obs", "gy", "gx"),
        P(("gx", "gy"), None),
        P(("gx", "gy")),
        P(("gx", "gy", "obs")),
        P(("gx", "gy", "obs")),
        P(("gx", "gy", "obs")),
        P(("gx", "gy", "obs")),
        P(("gx", "gy", "obs")),
        P(("gx", "gy", "obs")),
    )
    out_specs = (P(None, "obs", "gy", "gx"), P(("gx", "gy", "obs")))
    return jax.shard_map(
        per_device, mesh=mesh, in_specs=in_specs, out_specs=out_specs, check_vma=False
    )
```

profile of v0, /device:TPU:0, one launch (start us, length us, event | category | flops | bytes accessed | tf_op | source)
XLA Modules:
  0.0 398.3 jit_solution(8440060800442159052)
XLA Ops:
  4.2 3.2 scatter_custom_fusion
  7.3 5.2 %all-to-all-start = ((s32[8,1,128]{2,1,0:T(1,128)}), s32[8,1,128]{2,1,0:T(1,128)S(1)}, u32[]{:S(2)}, u32[]{:S(2)}) async-start(s32[8,1,128]{2,1,0:T(1,128)} %bitcast.14), calls=%async_computation | async-start | bytes 8192 | tf_op jit(solution)/shard_map/all_to_all | solution.py:95
  14.9 3.6 collective-permute-start.9
  20.6 137.4 %while.20 = (s32[]{:T(128)}, f32[4,1,128,128]{3,2,1,0:T(8,128)S(1)}, f32[1,130,130]{2,1,0:T(8,128)S(1)}, f32[1,130,130]{2,1,0:T(8,128)S(1)}, s32[]{:T(128)}) while((s32[]{:T(128)}, f32[4,1,128,128]{3,2,1,0:T(8,128)S(1)}, f32[1,130,130]{2,1,0:T(8,128)S(1)}, f32[1,130,130]{2,1,0:T(8,128)S(1)}, s32[]{:T(128)}) %tuple.66), condition=%wide.region_5.6_spmd, body=%wide.region_4.5_spmd.sunk | while | flops 1312802 | bytes 2155101 | solution.py:83
  22.1 5.8 %collective-permute-done = f32[4,1,128,1]{3,2,1,0:T(8,128)S(1)} collective-permute-done((f32[4,1,128,1]{3,2,1,0:T(8,128)S(1)}, f32[4,1,128,1]{3,2,1,0:T(8,128)S(1)}, u32[]{:S(2)}, u32[]{:S(2)}) %collective-permute-start) | collective-permute-done | bytes 2080 | tf_op jit(solution)/shard_map/while/body/eval_jaxpr/ppermute | solution.py:29
  27.9 2.8 collective-permute-done.1
  36.4 6.1 %collective-permute-done = f32[4,1,128,1]{3,2,1,0:T(8,128)S(1)} collective-permute-done((f32[4,1,128,1]{3,2,1,0:T(8,128)S(1)}, f32[4,1,128,1]{3,2,1,0:T(8,128)S(1)}, u32[]{:S(2)}, u32[]{:S(2)}) %collective-permute-start) | collective-permute-done | bytes 2080 | tf_op jit(solution)/shard_map/while/body/eval_jaxpr/ppermute | solution.py:29
  49.8 5.3 %collective-permute-done = f32[4,1,128,1]{3,2,1,0:T(8,128)S(1)} collective-permute-done((f32[4,1,128,1]{3,2,1,0:T(8,128)S(1)}, f32[4,1,128,1]{3,2,1,0:T(8,128)S(1)}, u32[]{:S(2)}, u32[]{:S(2)}) %collective-permute-start) | collective-permute-done | bytes 2080 | tf_op jit(solution)/shard_map/while/body/eval_jaxpr/ppermute | solution.py:29
  55.1 2.8 collective-permute-done.1
  63.6 6.1 %collective-permute-done = f32[4,1,128,1]{3,2,1,0:T(8,128)S(1)} collective-permute-done((f32[4,1,128,1]{3,2,1,0:T(8,128)S(1)}, f32[4,1,128,1]{3,2,1,0:T(8,128)S(1)}, u32[]{:S(2)}, u32[]{:S(2)}) %collective-permute-start) | collective-permute-done | bytes 2080 | tf_op jit(solution)/shard_map/while/body/eval_jaxpr/ppermute | solution.py:29
  77.1 5.3 %collective-permute-done = f32[4,1,128,1]{3,2,1,0:T(8,128)S(1)} collective-permute-done((f32[4,1,128,1]{3,2,1,0:T(8,128)S(1)}, f32[4,1,128,1]{3,2,1,0:T(8,128)S(1)}, u32[]{:S(2)}, u32[]{:S(2)}) %collective-permute-start) | collective-permute-done | bytes 2080 | tf_op jit(solution)/shard_map/while/body/eval_jaxpr/ppermute | solution.py:29
  82.3 2.8 collective-permute-done.1
  90.8 6.1 %collective-permute-done = f32[4,1,128,1]{3,2,1,0:T(8,128)S(1)} collective-permute-done((f32[4,1,128,1]{3,2,1,0:T(8,128)S(1)}, f32[4,1,128,1]{3,2,1,0:T(8,128)S(1)}, u32[]{:S(2)}, u32[]{:S(2)}) %collective-permute-start) | collective-permute-done | bytes 2080 | tf_op jit(solution)/shard_map/while/body/eval_jaxpr/ppermute | solution.py:29
  104.3 5.3 %collective-permute-done = f32[4,1,128,1]{3,2,1,0:T(8,128)S(1)} collective-permute-done((f32[4,1,128,1]{3,2,1,0:T(8,128)S(1)}, f32[4,1,128,1]{3,2,1,0:T(8,128)S(1)}, u32[]{:S(2)}, u32[]{:S(2)}) %collective-permute-start) | collective-permute-done | bytes 2080 | tf_op jit(solution)/shard_map/while/body/eval_jaxpr/ppermute | solution.py:29
  109.6 2.8 collective-permute-done.1
  118.0 6.1 %collective-permute-done = f32[4,1,128,1]{3,2,1,0:T(8,128)S(1)} collective-permute-done((f32[4,1,128,1]{3,2,1,0:T(8,128)S(1)}, f32[4,1,128,1]{3,2,1,0:T(8,128)S(1)}, u32[]{:S(2)}, u32[]{:S(2)}) %collective-permute-start) | collective-permute-done | bytes 2080 | tf_op jit(solution)/shard_map/while/body/eval_jaxpr/ppermute | solution.py:29
  131.5 5.3 %collective-permute-done = f32[4,1,128,1]{3,2,1,0:T(8,128)S(1)} collective-permute-done((f32[4,1,128,1]{3,2,1,0:T(8,128)S(1)}, f32[4,1,128,1]{3,2,1,0:T(8,128)S(1)}, u32[]{:S(2)}, u32[]{:S(2)}) %collective-permute-start) | collective-permute-done | bytes 2080 | tf_op jit(solution)/shard_map/while/body/eval_jaxpr/ppermute | solution.py:29
  136.8 2.8 collective-permute-done.1
  145.3 6.1 %collective-permute-done = f32[4,1,128,1]{3,2,1,0:T(8,128)S(1)} collective-permute-done((f32[4,1,128,1]{3,2,1,0:T(8,128)S(1)}, f32[4,1,128,1]{3,2,1,0:T(8,128)S(1)}, u32[]{:S(2)}, u32[]{:S(2)}) %collective-permute-start) | collective-permute-done | bytes 2080 | tf_op jit(solution)/shard_map/while/body/eval_jaxpr/ppermute | solution.py:29
  158.0 4.7 %copy.26 = f32[4,1,128,128]{0,3,2,1:T(8,128)} copy(f32[4,1,128,128]{3,2,1,0:T(8,128)S(1)} %get-tuple-element.46) | data formatting | bytes 524288 | tf_op jit(solution)/shard_map/while | solution.py:83
  162.7 6.2 %gather_fusion = f32[1024,4]{1,0:T(8,128)S(1)} fusion(f32[4,16384]{0,1:T(8,128)} %bitcast.73, s32[1024]{0:T(1024)S(1)} %fusion.34), kind=kCustom, calls=%fused_computation | custom fusion | bytes 36864 | tf_op jit(solution)/shard_map/jit(_take)/gather | solution.py:102
  169.7 3.3 all-to-all-start.1
  173.7 4.0 %all-to-all-done.1 = f32[8,4,128]{2,1,0:T(4,128)S(1)} async-done(((f32[8,4,128]{2,1,0:T(4,128)}), f32[8,4,128]{2,1,0:T(4,128)S(1)}, u32[]{:S(2)}, u32[]{:S(2)}) %all-to-all-start.1) | async-done | bytes 16416 | tf_op jit(solution)/shard_map/all_to_all | solution.py:104
  178.9 22.8 %all-gather = f32[4,2048]{0,1:T(8,128)S(1)} all-gather(f32[4,512]{0,1:T(8,128)S(1)} %bitcast.77), channel_id=2, replica_groups=mesh['gx'=4,'gy'=2,'obs'=4] {'obs'}, dimensions={1}, use_global_device_ids=true | all-gather | bytes 40960 | tf_op jit(solution)/shard_map/all_gather | solution.py:107
  202.0 3.1 gather_fusion.2
  205.2 3.1 gather_fusion.3
  208.4 3.3 scatter_custom_fusion.1
  211.7 3.4 scatter_fusion
  215.1 18.5 %all-reduce.2 = f32[4,4,512]{2,0,1:T(4,128)S(1)} all-reduce(f32[4,4,512]{2,0,1:T(4,128)S(1)} %copy.30), channel_id=3, replica_groups=mesh['gx'=4,'gy'=2,'obs'=4] {'obs'}, use_global_device_ids=true, to_apply=%region_8.9.clone | all-reduce | flops 8192 | bytes 65536
  237.0 3.3 all-to-all-start.2
  240.4 4.6 %all-to-all-done.2 = f32[8,4,128]{2,1,0:T(4,128)S(1)} async-done(((f32[8,4,128]{2,1,0:T(4,128)}), f32[8,4,128]{2,1,0:T(4,128)S(1)}, u32[]{:S(2)}, u32[]{:S(2)}) %all-to-all-start.2) | async-done | bytes 16416 | tf_op jit(solution)/shard_map/all_to_all | solution.py:126
  245.2 10.6 %scatter_custom_fusion.4 = f32[4,16384]{0,1:T(8,128)} fusion(s32[1024]{0:T(1024)S(1)} %bitcast.89, f32[1024,4]{1,0:T(8,128)S(1)} %copy.33, f32[]{:T(128)} %constant.17.clone.1), kind=kCustom, calls=%fused_computation.63 | custom fusion | flops 4096 | bytes 262148 | tf_op jit(solution)/shard_map/scatter-add | solution.py:129
  255.8 5.2 %copy.34 = f32[4,1,128,128]{3,2,1,0:T(8,128)S(1)} copy(f32[4,1,128,128]{0,3,2,1:T(8,128)} %bitcast.72) | data formatting | bytes 524288 | tf_op jit(solution)/shard_map/while | solution.py:83
  261.0 136.5 %while.21 = (s32[]{:T(128)}, f32[4,1,128,128]{3,2,1,0:T(8,128)S(1)}, f32[1,130,130]{2,1,0:T(8,128)S(1)}, f32[1,130,130]{2,1,0:T(8,128)S(1)}, s32[]{:T(128)}) while((s32[]{:T(128)}, f32[4,1,128,128]{3,2,1,0:T(8,128)S(1)}, f32[1,130,130]{2,1,0:T(8,128)S(1)}, f32[1,130,130]{2,1,0:T(8,128)S(1)}, s32[]{:T(128)}) %tuple.73), condition=%wide.region_12.13_spmd, body=%wide.region_11.12_spmd.sunk | while | flops 1312802 | bytes 2155101 | solution.py:83
  261.8 5.9 %collective-permute-done.4 = f32[4,1,128,1]{3,2,1,0:T(8,128)S(1)} collective-permute-done((f32[4,1,128,1]{3,2,1,0:T(8,128)S(1)}, f32[4,1,128,1]{3,2,1,0:T(8,128)S(1)}, u32[]{:S(2)}, u32[]{:S(2)}) %collective-permute-start.4) | collective-permute-done | bytes 2080 | tf_op jit(solution)/shard_map/while/body/eval_jaxpr/ppermute | solution.py:29
  275.1 5.5 %collective-permute-done.4 = f32[4,1,128,1]{3,2,1,0:T(8,128)S(1)} collective-permute-done((f32[4,1,128,1]{3,2,1,0:T(8,128)S(1)}, f32[4,1,128,1]{3,2,1,0:T(8,128)S(1)}, u32[]{:S(2)}, u32[]{:S(2)}) %collective-permute-start.4) | collective-permute-done | bytes 2080 | tf_op jit(solution)/shard_map/while/body/eval_jaxpr/ppermute | solution.py:29
  289.4 5.4 %collective-permute-done.4 = f32[4,1,128,1]{3,2,1,0:T(8,128)S(1)} collective-permute-done((f32[4,1,128,1]{3,2,1,0:T(8,128)S(1)}, f32[4,1,128,1]{3,2,1,0:T(8,128)S(1)}, u32[]{:S(2)}, u32[]{:S(2)}) %collective-permute-start.4) | collective-permute-done | bytes 2080 | tf_op jit(solution)/shard_map/while/body/eval_jaxpr/ppermute | solution.py:29
  294.8 2.5 collective-permute-done.5
  302.4 5.5 %collective-permute-done.4 = f32[4,1,128,1]{3,2,1,0:T(8,128)S(1)} collective-permute-done((f32[4,1,128,1]{3,2,1,0:T(8,128)S(1)}, f32[4,1,128,1]{3,2,1,0:T(8,128)S(1)}, u32[]{:S(2)}, u32[]{:S(2)}) %collective-permute-start.4) | collective-permute-done | bytes 2080 | tf_op jit(solution)/shard_map/while/body/eval_jaxpr/ppermute | solution.py:29
  316.6 5.4 %collective-permute-done.4 = f32[4,1,128,1]{3,2,1,0:T(8,128)S(1)} collective-permute-done((f32[4,1,128,1]{3,2,1,0:T(8,128)S(1)}, f32[4,1,128,1]{3,2,1,0:T(8,128)S(1)}, u32[]{:S(2)}, u32[]{:S(2)}) %collective-permute-start.4) | collective-permute-done | bytes 2080 | tf_op jit(solution)/shard_map/while/body/eval_jaxpr/ppermute | solution.py:29
  322.1 2.5 collective-permute-done.5
  329.6 5.5 %collective-permute-done.4 = f32[4,1,128,1]{3,2,1,0:T(8,128)S(1)} collective-permute-done((f32[4,1,128,1]{3,2,1,0:T(8,128)S(1)}, f32[4,1,128,1]{3,2,1,0:T(8,128)S(1)}, u32[]{:S(2)}, u32[]{:S(2)}) %collective-permute-start.4) | collective-permute-done | bytes 2080 | tf_op jit(solution)/shard_map/while/body/eval_jaxpr/ppermute | solution.py:29
  343.8 5.4 %collective-permute-done.4 = f32[4,1,128,1]{3,2,1,0:T(8,128)S(1)} collective-permute-done((f32[4,1,128,1]{3,2,1,0:T(8,128)S(1)}, f32[4,1,128,1]{3,2,1,0:T(8,128)S(1)}, u32[]{:S(2)}, u32[]{:S(2)}) %collective-permute-start.4) | collective-permute-done | bytes 2080 | tf_op jit(solution)/shard_map/while/body/eval_jaxpr/ppermute | solution.py:29
  349.3 2.5 collective-permute-done.5
  356.8 5.5 %collective-permute-done.4 = f32[4,1,128,1]{3,2,1,0:T(8,128)S(1)} collective-permute-done((f32[4,1,128,1]{3,2,1,0:T(8,128)S(1)}, f32[4,1,128,1]{3,2,1,0:T(8,128)S(1)}, u32[]{:S(2)}, u32[]{:S(2)}) %collective-permute-start.4) | collective-permute-done | bytes 2080 | tf_op jit(solution)/shard_map/while/body/eval_jaxpr/ppermute | solution.py:29
  371.1 5.4 %collective-permute-done.4 = f32[4,1,128,1]{3,2,1,0:T(8,128)S(1)} collective-permute-done((f32[4,1,128,1]{3,2,1,0:T(8,128)S(1)}, f32[4,1,128,1]{3,2,1,0:T(8,128)S(1)}, u32[]{:S(2)}, u32[]{:S(2)}) %collective-permute-start.4) | collective-permute-done | bytes 2080 | tf_op jit(solution)/shard_map/while/body/eval_jaxpr/ppermute | solution.py:29
  376.5 2.5 collective-permute-done.5
  384.0 5.5 %collective-permute-done.4 = f32[4,1,128,1]{3,2,1,0:T(8,128)S(1)} collective-permute-done((f32[4,1,128,1]{3,2,1,0:T(8,128)S(1)}, f32[4,1,128,1]{3,2,1,0:T(8,128)S(1)}, u32[]{:S(2)}, u32[]{:S(2)}) %collective-permute-start.4) | collective-permute-done | bytes 2080 | tf_op jit(solution)/shard_map/while/body/eval_jaxpr/ppermute | solution.py:29
  (288 shorter events, 151.2 us)
Async XLA Ops:
  7.3 155.4 %all-to-all-start = ((s32[8,1,128]{2,1,0:T(1,128)}), s32[8,1,128]{2,1,0:T(1,128)S(1)}, u32[]{:S(2)}, u32[]{:S(2)}) async-start(s32[8,1,128]{2,1,0:T(1,128)} %bitcast.14), calls=%async_computation | async-start | bytes 8192 | tf_op jit(solution)/shard_map/all_to_all | solution.py:95
  13.4 6.8 %collective-permute-start.8 = (f32[1,128,1]{2,1,0:T(8,128)S(1)}, f32[1,128,1]{2,1,0:T(8,128)S(1)}, u32[]{:S(2)}, u32[]{:S(2)}) collective-permute-start(f32[1,128,1]{2,1,0:T(8,128)S(1)} %slice.113), channel_id=1, source_target_pairs={{0,8},{8,16},{16,24},{24,0},{1,9},{9,17},{17,25},{25,1},{2,10},{10... | collective-permute-start | bytes 1544 | tf_op jit(solution)/shard_map/ppermute | solution.py:11
  14.9 5.5 %collective-permute-start.9 = (f32[1,1,128]{2,1,0:T(1,128)S(1)}, f32[1,1,128]{2,1,0:T(1,128)S(1)}, u32[]{:S(2)}, u32[]{:S(2)}) collective-permute-start(f32[1,1,128]{2,1,0:T(1,128)S(1)} %slice.114), channel_id=1, source_target_pairs={{0,4},{1,5},{2,6},{3,7},{8,12},{9,13},{10,14},{11,15},{16,20},{17,... | collective-permute-start | bytes 1544 | tf_op jit(solution)/shard_map/ppermute | solution.py:17
  20.7 7.2 %collective-permute-start = (f32[4,1,128,1]{3,2,1,0:T(8,128)S(1)}, f32[4,1,128,1]{3,2,1,0:T(8,128)S(1)}, u32[]{:S(2)}, u32[]{:S(2)}) collective-permute-start(f32[4,1,128,1]{3,2,1,0:T(8,128)S(1)} %get-tuple-element.168), channel_id=1, source_target_pairs={{8,0},{16,8},{24,16},{0,24},{9,1},{17,9},{25,17},{1,25},{10,2},{18... | collective-permute-start | bytes 6152 | tf_op jit(solution)/shard_map/while/body/eval_jaxpr/ppermute | solution.py:29
  22.1 8.6 %collective-permute-start.1 = (f32[4,1,128,1]{3,2,1,0:T(8,128)S(1)}, f32[4,1,128,1]{3,2,1,0:T(8,128)S(1)}, u32[]{:S(2)}, u32[]{:S(2)}) collective-permute-start(f32[4,1,128,1]{3,2,1,0:T(8,128)S(1)} %get-tuple-element.169), channel_id=1, source_target_pairs={{0,8},{8,16},{16,24},{24,0},{1,9},{9,17},{17,25},{25,1},{2,10},{10... | collective-permute-start | bytes 6152 | tf_op jit(solution)/shard_map/while/body/eval_jaxpr/ppermute | solution.py:26
  35.8 6.7 %collective-permute-start = (f32[4,1,128,1]{3,2,1,0:T(8,128)S(1)}, f32[4,1,128,1]{3,2,1,0:T(8,128)S(1)}, u32[]{:S(2)}, u32[]{:S(2)}) collective-permute-start(f32[4,1,128,1]{3,2,1,0:T(8,128)S(1)} %get-tuple-element.168), channel_id=1, source_target_pairs={{8,0},{16,8},{24,16},{0,24},{9,1},{17,9},{25,17},{1,25},{10,2},{18... | collective-permute-start | bytes 6152 | tf_op jit(solution)/shard_map/while/body/eval_jaxpr/ppermute | solution.py:29
  35.9 7.7 %collective-permute-start.1 = (f32[4,1,128,1]{3,2,1,0:T(8,128)S(1)}, f32[4,1,128,1]{3,2,1,0:T(8,128)S(1)}, u32[]{:S(2)}, u32[]{:S(2)}) collective-permute-start(f32[4,1,128,1]{3,2,1,0:T(8,128)S(1)} %get-tuple-element.169), channel_id=1, source_target_pairs={{0,8},{8,16},{16,24},{24,0},{1,9},{9,17},{17,25},{25,1},{2,10},{10... | collective-permute-start | bytes 6152 | tf_op jit(solution)/shard_map/while/body/eval_jaxpr/ppermute | solution.py:26
  49.3 5.8 %collective-permute-start = (f32[4,1,128,1]{3,2,1,0:T(8,128)S(1)}, f32[4,1,128,1]{3,2,1,0:T(8,128)S(1)}, u32[]{:S(2)}, u32[]{:S(2)}) collective-permute-start(f32[4,1,128,1]{3,2,1,0:T(8,128)S(1)} %get-tuple-element.168), channel_id=1, source_target_pairs={{8,0},{16,8},{24,16},{0,24},{9,1},{17,9},{25,17},{1,25},{10,2},{18... | collective-permute-start | bytes 6152 | tf_op jit(solution)/shard_map/while/body/eval_jaxpr/ppermute | solution.py:29
  49.3 8.6 %collective-permute-start.1 = (f32[4,1,128,1]{3,2,1,0:T(8,128)S(1)}, f32[4,1,128,1]{3,2,1,0:T(8,128)S(1)}, u32[]{:S(2)}, u32[]{:S(2)}) collective-permute-start(f32[4,1,128,1]{3,2,1,0:T(8,128)S(1)} %get-tuple-element.169), channel_id=1, source_target_pairs={{0,8},{8,16},{16,24},{24,0},{1,9},{9,17},{17,25},{25,1},{2,10},{10... | collective-permute-start | bytes 6152 | tf_op jit(solution)/shard_map/while/body/eval_jaxpr/ppermute | solution.py:26
  63.0 6.7 %collective-permute-start = (f32[4,1,128,1]{3,2,1,0:T(8,128)S(1)}, f32[4,1,128,1]{3,2,1,0:T(8,128)S(1)}, u32[]{:S(2)}, u32[]{:S(2)}) collective-permute-start(f32[4,1,128,1]{3,2,1,0:T(8,128)S(1)} %get-tuple-element.168), channel_id=1, source_target_pairs={{8,0},{16,8},{24,16},{0,24},{9,1},{17,9},{25,17},{1,25},{10,2},{18... | collective-permute-start | bytes 6152 | tf_op jit(solution)/shard_map/while/body/eval_jaxpr/ppermute | solution.py:29
  63.1 7.7 %collective-permute-start.1 = (f32[4,1,128,1]{3,2,1,0:T(8,128)S(1)}, f32[4,1,128,1]{3,2,1,0:T(8,128)S(1)}, u32[]{:S(2)}, u32[]{:S(2)}) collective-permute-start(f32[4,1,128,1]{3,2,1,0:T(8,128)S(1)} %get-tuple-element.169), channel_id=1, source_target_pairs={{0,8},{8,16},{16,24},{24,0},{1,9},{9,17},{17,25},{25,1},{2,10},{10... | collective-permute-start | bytes 6152 | tf_op jit(solution)/shard_map/while/body/eval_jaxpr/ppermute | solution.py:26
  76.5 5.8 %collective-permute-start = (f32[4,1,128,1]{3,2,1,0:T(8,128)S(1)}, f32[4,1,128,1]{3,2,1,0:T(8,128)S(1)}, u32[]{:S(2)}, u32[]{:S(2)}) collective-permute-start(f32[4,1,128,1]{3,2,1,0:T(8,128)S(1)} %get-tuple-element.168), channel_id=1, source_target_pairs={{8,0},{16,8},{24,16},{0,24},{9,1},{17,9},{25,17},{1,25},{10,2},{18... | collective-permute-start | bytes 6152 | tf_op jit(solution)/shard_map/while/body/eval_jaxpr/ppermute | solution.py:29
  76.6 8.6 %collective-permute-start.1 = (f32[4,1,128,1]{3,2,1,0:T(8,128)S(1)}, f32[4,1,128,1]{3,2,1,0:T(8,128)S(1)}, u32[]{:S(2)}, u32[]{:S(2)}) collective-permute-start(f32[4,1,128,1]{3,2,1,0:T(8,128)S(1)} %get-tuple-element.169), channel_id=1, source_target_pairs={{0,8},{8,16},{16,24},{24,0},{1,9},{9,17},{17,25},{25,1},{2,10},{10... | collective-permute-start | bytes 6152 | tf_op jit(solution)/shard_map/while/body/eval_jaxpr/ppermute | solution.py:26
  90.3 6.7 %collective-permute-start = (f32[4,1,128,1]{3,2,1,0:T(8,128)S(1)}, f32[4,1,128,1]{3,2,1,0:T(8,128)S(1)}, u32[]{:S(2)}, u32[]{:S(2)}) collective-permute-start(f32[4,1,128,1]{3,2,1,0:T(8,128)S(1)} %get-tuple-element.168), channel_id=1, source_target_pairs={{8,0},{16,8},{24,16},{0,24},{9,1},{17,9},{25,17},{1,25},{10,2},{18... | collective-permute-start | bytes 6152 | tf_op jit(solution)/shard_map/while/body/eval_jaxpr/ppermute | solution.py:29
  90.3 7.7 %collective-permute-start.1 = (f32[4,1,128,1]{3,2,1,0:T(8,128)S(1)}, f32[4,1,128,1]{3,2,1,0:T(8,128)S(1)}, u32[]{:S(2)}, u32[]{:S(2)}) collective-permute-start(f32[4,1,128,1]{3,2,1,0:T(8,128)S(1)} %get-tuple-element.169), channel_id=1, source_target_pairs={{0,8},{8,16},{16,24},{24,0},{1,9},{9,17},{17,25},{25,1},{2,10},{10... | collective-permute-start | bytes 6152 | tf_op jit(solution)/shard_map/while/body/eval_jaxpr/ppermute | solution.py:26
  103.7 5.8 %collective-permute-start = (f32[4,1,128,1]{3,2,1,0:T(8,128)S(1)}, f32[4,1,128,1]{3,2,1,0:T(8,128)S(1)}, u32[]{:S(2)}, u32[]{:S(2)}) collective-permute-start(f32[4,1,128,1]{3,2,1,0:T(8,128)S(1)} %get-tuple-element.168), channel_id=1, source_target_pairs={{8,0},{16,8},{24,16},{0,24},{9,1},{17,9},{25,17},{1,25},{10,2},{18... | collective-permute-start | bytes 6152 | tf_op jit(solution)/shard_map/while/body/eval_jaxpr/ppermute | solution.py:29
  103.8 8.6 %collective-permute-start.1 = (f32[4,1,128,1]{3,2,1,0:T(8,128)S(1)}, f32[4,1,128,1]{3,2,1,0:T(8,128)S(1)}, u32[]{:S(2)}, u32[]{:S(2)}) collective-permute-start(f32[4,1,128,1]{3,2,1,0:T(8,128)S(1)} %get-tuple-element.169), channel_id=1, source_target_pairs={{0,8},{8,16},{16,24},{24,0},{1,9},{9,17},{17,25},{25,1},{2,10},{10... | collective-permute-start | bytes 6152 | tf_op jit(solution)/shard_map/while/body/eval_jaxpr/ppermute | solution.py:26
  117.5 6.7 %collective-permute-start = (f32[4,1,128,1]{3,2,1,0:T(8,128)S(1)}, f32[4,1,128,1]{3,2,1,0:T(8,128)S(1)}, u32[]{:S(2)}, u32[]{:S(2)}) collective-permute-start(f32[4,1,128,1]{3,2,1,0:T(8,128)S(1)} %get-tuple-element.168), channel_id=1, source_target_pairs={{8,0},{16,8},{24,16},{0,24},{9,1},{17,9},{25,17},{1,25},{10,2},{18... | collective-permute-start | bytes 6152 | tf_op jit(solution)/shard_map/while/body/eval_jaxpr/ppermute | solution.py:29
  117.5 7.7 %collective-permute-start.1 = (f32[4,1,128,1]{3,2,1,0:T(8,128)S(1)}, f32[4,1,128,1]{3,2,1,0:T(8,128)S(1)}, u32[]{:S(2)}, u32[]{:S(2)}) collective-permute-start(f32[4,1,128,1]{3,2,1,0:T(8,128)S(1)} %get-tuple-element.169), channel_id=1, source_target_pairs={{0,8},{8,16},{16,24},{24,0},{1,9},{9,17},{17,25},{25,1},{2,10},{10... | collective-permute-start | bytes 6152 | tf_op jit(solution)/shard_map/while/body/eval_jaxpr/ppermute | solution.py:26
  130.9 5.8 %collective-permute-start = (f32[4,1,128,1]{3,2,1,0:T(8,128)S(1)}, f32[4,1,128,1]{3,2,1,0:T(8,128)S(1)}, u32[]{:S(2)}, u32[]{:S(2)}) collective-permute-start(f32[4,1,128,1]{3,2,1,0:T(8,128)S(1)} %get-tuple-element.168), channel_id=1, source_target_pairs={{8,0},{16,8},{24,16},{0,24},{9,1},{17,9},{25,17},{1,25},{10,2},{18... | collective-permute-start | bytes 6152 | tf_op jit(solution)/shard_map/while/body/eval_jaxpr/ppermute | solution.py:29
  131.0 8.6 %collective-permute-start.1 = (f32[4,1,128,1]{3,2,1,0:T(8,128)S(1)}, f32[4,1,128,1]{3,2,1,0:T(8,128)S(1)}, u32[]{:S(2)}, u32[]{:S(2)}) collective-permute-start(f32[4,1,128,1]{3,2,1,0:T(8,128)S(1)} %get-tuple-element.169), channel_id=1, source_target_pairs={{0,8},{8,16},{16,24},{24,0},{1,9},{9,17},{17,25},{25,1},{2,10},{10... | collective-permute-start | bytes 6152 | tf_op jit(solution)/shard_map/while/body/eval_jaxpr/ppermute | solution.py:26
  144.7 6.7 %collective-permute-start = (f32[4,1,128,1]{3,2,1,0:T(8,128)S(1)}, f32[4,1,128,1]{3,2,1,0:T(8,128)S(1)}, u32[]{:S(2)}, u32[]{:S(2)}) collective-permute-start(f32[4,1,128,1]{3,2,1,0:T(8,128)S(1)} %get-tuple-element.168), channel_id=1, source_target_pairs={{8,0},{16,8},{24,16},{0,24},{9,1},{17,9},{25,17},{1,25},{10,2},{18... | collective-permute-start | bytes 6152 | tf_op jit(solution)/shard_map/while/body/eval_jaxpr/ppermute | solution.py:29
  144.8 7.7 %collective-permute-start.1 = (f32[4,1,128,1]{3,2,1,0:T(8,128)S(1)}, f32[4,1,128,1]{3,2,1,0:T(8,128)S(1)}, u32[]{:S(2)}, u32[]{:S(2)}) collective-permute-start(f32[4,1,128,1]{3,2,1,0:T(8,128)S(1)} %get-tuple-element.169), channel_id=1, source_target_pairs={{0,8},{8,16},{16,24},{24,0},{1,9},{9,17},{17,25},{25,1},{2,10},{10... | collective-permute-start | bytes 6152 | tf_op jit(solution)/shard_map/while/body/eval_jaxpr/ppermute | solution.py:26
  169.7 8.0 %all-to-all-start.1 = ((f32[8,4,128]{2,1,0:T(4,128)}), f32[8,4,128]{2,1,0:T(4,128)S(1)}, u32[]{:S(2)}, u32[]{:S(2)}) async-start(f32[8,4,128]{2,1,0:T(4,128)} %select_bitcast_fusion), calls=%async_computation.1 | async-start | bytes 32768 | tf_op jit(solution)/shard_map/all_to_all | solution.py:104
  237.0 8.0 %all-to-all-start.2 = ((f32[8,4,128]{2,1,0:T(4,128)}), f32[8,4,128]{2,1,0:T(4,128)S(1)}, u32[]{:S(2)}, u32[]{:S(2)}) async-start(f32[8,4,128]{2,1,0:T(4,128)} %bitcast.32), calls=%async_computation.2 | async-start | bytes 32768 | tf_op jit(solution)/shard_map/all_to_all | solution.py:126
  261.2 6.5 %collective-permute-start.4 = (f32[4,1,128,1]{3,2,1,0:T(8,128)S(1)}, f32[4,1,128,1]{3,2,1,0:T(8,128)S(1)}, u32[]{:S(2)}, u32[]{:S(2)}) collective-permute-start(f32[4,1,128,1]{3,2,1,0:T(8,128)S(1)} %get-tuple-element.180), channel_id=1, source_target_pairs={{8,0},{16,8},{24,16},{0,24},{9,1},{17,9},{25,17},{1,25},{10,2},{18... | collective-permute-start | bytes 6152 | tf_op jit(solution)/shard_map/while/body/eval_jaxpr/ppermute | solution.py:29
  261.7 8.5 %collective-permute-start.5 = (f32[4,1,128,1]{3,2,1,0:T(8,128)S(1)}, f32[4,1,128,1]{3,2,1,0:T(8,128)S(1)}, u32[]{:S(2)}, u32[]{:S(2)}) collective-permute-start(f32[4,1,128,1]{3,2,1,0:T(8,128)S(1)} %get-tuple-element.181), channel_id=1, source_target_pairs={{0,8},{8,16},{16,24},{24,0},{1,9},{9,17},{17,25},{25,1},{2,10},{10... | collective-permute-start | bytes 6152 | tf_op jit(solution)/shard_map/while/body/eval_jaxpr/ppermute | solution.py:26
  270.2 3.7 collective-permute-start.6
  274.6 6.1 %collective-permute-start.4 = (f32[4,1,128,1]{3,2,1,0:T(8,128)S(1)}, f32[4,1,128,1]{3,2,1,0:T(8,128)S(1)}, u32[]{:S(2)}, u32[]{:S(2)}) collective-permute-start(f32[4,1,128,1]{3,2,1,0:T(8,128)S(1)} %get-tuple-element.180), channel_id=1, source_target_pairs={{8,0},{16,8},{24,16},{0,24},{9,1},{17,9},{25,17},{1,25},{10,2},{18... | collective-permute-start | bytes 6152 | tf_op jit(solution)/shard_map/while/body/eval_jaxpr/ppermute | solution.py:29
  274.6 8.4 %collective-permute-start.5 = (f32[4,1,128,1]{3,2,1,0:T(8,128)S(1)}, f32[4,1,128,1]{3,2,1,0:T(8,128)S(1)}, u32[]{:S(2)}, u32[]{:S(2)}) collective-permute-start(f32[4,1,128,1]{3,2,1,0:T(8,128)S(1)} %get-tuple-element.181), channel_id=1, source_target_pairs={{0,8},{8,16},{16,24},{24,0},{1,9},{9,17},{17,25},{25,1},{2,10},{10... | collective-permute-start | bytes 6152 | tf_op jit(solution)/shard_map/while/body/eval_jaxpr/ppermute | solution.py:26
  288.8 6.0 %collective-permute-start.4 = (f32[4,1,128,1]{3,2,1,0:T(8,128)S(1)}, f32[4,1,128,1]{3,2,1,0:T(8,128)S(1)}, u32[]{:S(2)}, u32[]{:S(2)}) collective-permute-start(f32[4,1,128,1]{3,2,1,0:T(8,128)S(1)} %get-tuple-element.180), channel_id=1, source_target_pairs={{8,0},{16,8},{24,16},{0,24},{9,1},{17,9},{25,17},{1,25},{10,2},{18... | collective-permute-start | bytes 6152 | tf_op jit(solution)/shard_map/while/body/eval_jaxpr/ppermute | solution.py:29
  288.9 8.5 %collective-permute-start.5 = (f32[4,1,128,1]{3,2,1,0:T(8,128)S(1)}, f32[4,1,128,1]{3,2,1,0:T(8,128)S(1)}, u32[]{:S(2)}, u32[]{:S(2)}) collective-permute-start(f32[4,1,128,1]{3,2,1,0:T(8,128)S(1)} %get-tuple-element.181), channel_id=1, source_target_pairs={{0,8},{8,16},{16,24},{24,0},{1,9},{9,17},{17,25},{25,1},{2,10},{10... | collective-permute-start | bytes 6152 | tf_op jit(solution)/shard_map/while/body/eval_jaxpr/ppermute | solution.py:26
  297.4 3.7 collective-permute-start.6
  301.8 6.1 %collective-permute-start.4 = (f32[4,1,128,1]{3,2,1,0:T(8,128)S(1)}, f32[4,1,128,1]{3,2,1,0:T(8,128)S(1)}, u32[]{:S(2)}, u32[]{:S(2)}) collective-permute-start(f32[4,1,128,1]{3,2,1,0:T(8,128)S(1)} %get-tuple-element.180), channel_id=1, source_target_pairs={{8,0},{16,8},{24,16},{0,24},{9,1},{17,9},{25,17},{1,25},{10,2},{18... | collective-permute-start | bytes 6152 | tf_op jit(solution)/shard_map/while/body/eval_jaxpr/ppermute | solution.py:29
  301.9 8.4 %collective-permute-start.5 = (f32[4,1,128,1]{3,2,1,0:T(8,128)S(1)}, f32[4,1,128,1]{3,2,1,0:T(8,128)S(1)}, u32[]{:S(2)}, u32[]{:S(2)}) collective-permute-start(f32[4,1,128,1]{3,2,1,0:T(8,128)S(1)} %get-tuple-element.181), channel_id=1, source_target_pairs={{0,8},{8,16},{16,24},{24,0},{1,9},{9,17},{17,25},{25,1},{2,10},{10... | collective-permute-start | bytes 6152 | tf_op jit(solution)/shard_map/while/body/eval_jaxpr/ppermute | solution.py:26
  316.1 6.0 %collective-permute-start.4 = (f32[4,1,128,1]{3,2,1,0:T(8,128)S(1)}, f32[4,1,128,1]{3,2,1,0:T(8,128)S(1)}, u32[]{:S(2)}, u32[]{:S(2)}) collective-permute-start(f32[4,1,128,1]{3,2,1,0:T(8,128)S(1)} %get-tuple-element.180), channel_id=1, source_target_pairs={{8,0},{16,8},{24,16},{0,24},{9,1},{17,9},{25,17},{1,25},{10,2},{18... | collective-permute-start | bytes 6152 | tf_op jit(solution)/shard_map/while/body/eval_jaxpr/ppermute | solution.py:29
  316.1 8.5 %collective-permute-start.5 = (f32[4,1,128,1]{3,2,1,0:T(8,128)S(1)}, f32[4,1,128,1]{3,2,1,0:T(8,128)S(1)}, u32[]{:S(2)}, u32[]{:S(2)}) collective-permute-start(f32[4,1,128,1]{3,2,1,0:T(8,128)S(1)} %get-tuple-element.181), channel_id=1, source_target_pairs={{0,8},{8,16},{16,24},{24,0},{1,9},{9,17},{17,25},{25,1},{2,10},{10... | collective-permute-start | bytes 6152 | tf_op jit(solution)/shard_map/while/body/eval_jaxpr/ppermute | solution.py:26
  324.7 3.7 collective-permute-start.6
  329.0 6.1 %collective-permute-start.4 = (f32[4,1,128,1]{3,2,1,0:T(8,128)S(1)}, f32[4,1,128,1]{3,2,1,0:T(8,128)S(1)}, u32[]{:S(2)}, u32[]{:S(2)}) collective-permute-start(f32[4,1,128,1]{3,2,1,0:T(8,128)S(1)} %get-tuple-element.180), channel_id=1, source_target_pairs={{8,0},{16,8},{24,16},{0,24},{9,1},{17,9},{25,17},{1,25},{10,2},{18... | collective-permute-start | bytes 6152 | tf_op jit(solution)/shard_map/while/body/eval_jaxpr/ppermute | solution.py:29
  329.1 8.4 %collective-permute-start.5 = (f32[4,1,128,1]{3,2,1,0:T(8,128)S(1)}, f32[4,1,128,1]{3,2,1,0:T(8,128)S(1)}, u32[]{:S(2)}, u32[]{:S(2)}) collective-permute-start(f32[4,1,128,1]{3,2,1,0:T(8,128)S(1)} %get-tuple-element.181), channel_id=1, source_target_pairs={{0,8},{8,16},{16,24},{24,0},{1,9},{9,17},{17,25},{25,1},{2,10},{10... | collective-permute-start | bytes 6152 | tf_op jit(solution)/shard_map/while/body/eval_jaxpr/ppermute | solution.py:26
  343.3 6.0 %collective-permute-start.4 = (f32[4,1,128,1]{3,2,1,0:T(8,128)S(1)}, f32[4,1,128,1]{3,2,1,0:T(8,128)S(1)}, u32[]{:S(2)}, u32[]{:S(2)}) collective-permute-start(f32[4,1,128,1]{3,2,1,0:T(8,128)S(1)} %get-tuple-element.180), channel_id=1, source_target_pairs={{8,0},{16,8},{24,16},{0,24},{9,1},{17,9},{25,17},{1,25},{10,2},{18... | collective-permute-start | bytes 6152 | tf_op jit(solution)/shard_map/while/body/eval_jaxpr/ppermute | solution.py:29
  343.3 8.5 %collective-permute-start.5 = (f32[4,1,128,1]{3,2,1,0:T(8,128)S(1)}, f32[4,1,128,1]{3,2,1,0:T(8,128)S(1)}, u32[]{:S(2)}, u32[]{:S(2)}) collective-permute-start(f32[4,1,128,1]{3,2,1,0:T(8,128)S(1)} %get-tuple-element.181), channel_id=1, source_target_pairs={{0,8},{8,16},{16,24},{24,0},{1,9},{9,17},{17,25},{25,1},{2,10},{10... | collective-permute-start | bytes 6152 | tf_op jit(solution)/shard_map/while/body/eval_jaxpr/ppermute | solution.py:26
  356.2 6.1 %collective-permute-start.4 = (f32[4,1,128,1]{3,2,1,0:T(8,128)S(1)}, f32[4,1,128,1]{3,2,1,0:T(8,128)S(1)}, u32[]{:S(2)}, u32[]{:S(2)}) collective-permute-start(f32[4,1,128,1]{3,2,1,0:T(8,128)S(1)} %get-tuple-element.180), channel_id=1, source_target_pairs={{8,0},{16,8},{24,16},{0,24},{9,1},{17,9},{25,17},{1,25},{10,2},{18... | collective-permute-start | bytes 6152 | tf_op jit(solution)/shard_map/while/body/eval_jaxpr/ppermute | solution.py:29
  356.3 8.4 %collective-permute-start.5 = (f32[4,1,128,1]{3,2,1,0:T(8,128)S(1)}, f32[4,1,128,1]{3,2,1,0:T(8,128)S(1)}, u32[]{:S(2)}, u32[]{:S(2)}) collective-permute-start(f32[4,1,128,1]{3,2,1,0:T(8,128)S(1)} %get-tuple-element.181), channel_id=1, source_target_pairs={{0,8},{8,16},{16,24},{24,0},{1,9},{9,17},{17,25},{25,1},{2,10},{10... | collective-permute-start | bytes 6152 | tf_op jit(solution)/shard_map/while/body/eval_jaxpr/ppermute | solution.py:26
  370.5 6.0 %collective-permute-start.4 = (f32[4,1,128,1]{3,2,1,0:T(8,128)S(1)}, f32[4,1,128,1]{3,2,1,0:T(8,128)S(1)}, u32[]{:S(2)}, u32[]{:S(2)}) collective-permute-start(f32[4,1,128,1]{3,2,1,0:T(8,128)S(1)} %get-tuple-element.180), channel_id=1, source_target_pairs={{8,0},{16,8},{24,16},{0,24},{9,1},{17,9},{25,17},{1,25},{10,2},{18... | collective-permute-start | bytes 6152 | tf_op jit(solution)/shard_map/while/body/eval_jaxpr/ppermute | solution.py:29
  370.6 8.5 %collective-permute-start.5 = (f32[4,1,128,1]{3,2,1,0:T(8,128)S(1)}, f32[4,1,128,1]{3,2,1,0:T(8,128)S(1)}, u32[]{:S(2)}, u32[]{:S(2)}) collective-permute-start(f32[4,1,128,1]{3,2,1,0:T(8,128)S(1)} %get-tuple-element.181), channel_id=1, source_target_pairs={{0,8},{8,16},{16,24},{24,0},{1,9},{9,17},{17,25},{25,1},{2,10},{10... | collective-permute-start | bytes 6152 | tf_op jit(solution)/shard_map/while/body/eval_jaxpr/ppermute | solution.py:26
  383.5 6.1 %collective-permute-start.4 = (f32[4,1,128,1]{3,2,1,0:T(8,128)S(1)}, f32[4,1,128,1]{3,2,1,0:T(8,128)S(1)}, u32[]{:S(2)}, u32[]{:S(2)}) collective-permute-start(f32[4,1,128,1]{3,2,1,0:T(8,128)S(1)} %get-tuple-element.180), channel_id=1, source_target_pairs={{8,0},{16,8},{24,16},{0,24},{9,1},{17,9},{25,17},{1,25},{10,2},{18... | collective-permute-start | bytes 6152 | tf_op jit(solution)/shard_map/while/body/eval_jaxpr/ppermute | solution.py:29
  383.5 8.4 %collective-permute-start.5 = (f32[4,1,128,1]{3,2,1,0:T(8,128)S(1)}, f32[4,1,128,1]{3,2,1,0:T(8,128)S(1)}, u32[]{:S(2)}, u32[]{:S(2)}) collective-permute-start(f32[4,1,128,1]{3,2,1,0:T(8,128)S(1)} %get-tuple-element.181), channel_id=1, source_target_pairs={{0,8},{8,16},{16,24},{24,0},{1,9},{9,17},{17,25},{25,1},{2,10},{10... | collective-permute-start | bytes 6152 | tf_op jit(solution)/shard_map/while/body/eval_jaxpr/ppermute | solution.py:26
  (43 other events, 490.0 us)
where the time goes:
time: 399 us; the launch traced here: 398 us
  waiting for transfers between devices  212 us (53%)
  starting transfers between devices  69.7 us (17%)
  blocking collectives  41.3 us (10%)
  local copies, waits for them, and re-layouts  39 us (10%)
  other arithmetic  33.9 us (8%)
    ppermute x40, waiting for transfers between devices, with_halo(): lax.ppermute(lax.slice_in_dim(block, 0, width, axis=dim), axis, backward)  130 us
    ppermute x40, waiting for transfers between devices, with_halo(): lax.ppermute(lax.slice_in_dim(block, block.shape[dim] - width, None, axis...  73.2 us
    ppermute x40, starting transfers between devices, with_halo(): lax.ppermute(lax.slice_in_dim(block, block.shape[dim] - width, None, axis...  27.9 us
    ppermute x40, starting transfers between devices, with_halo(): lax.ppermute(lax.slice_in_dim(block, 0, width, axis=dim), axis, backward)  25.8 us
    all_gather x1, blocking collectives, per_device(): columns = lax.all_gather(slab, 'obs', axis=1, tiled=True)  22.8 us
    unnamed x1, blocking collectives  18.5 us
    scatter-add x1, other arithmetic, per_device(): jnp.zeros((flat_levels, lat_cells * lon_cells), jnp.float32).at[:, cells]  10.6 us
    while x2, local copies, waits for them, and re-layouts, diffuse(): return lax.fori_loop(0, STEPS, sweep, field)  9.9 us
  transfers between devices with their start and end apart: 85, of which 82 were waited for; matrix products, arithmetic and copies ran while one was open for 5% of the time, Pallas kernels for 0%

commit v1 on v0

v1 whole, which is shorter than its diff:
```python
import functools

import jax
import jax.numpy as jnp
from jax import lax
from jax.experimental import pallas as pl
from jax.experimental.pallas import tpu as pltpu
from jax.sharding import PartitionSpec as P

STEPS = 10
HALO = 16
LANES = 128
GROUP = 8
CHUNK = 8
MESH = pl.DeviceIdType.MESH


def halves(value, size):
    if size & (size - 1) == 0:
        return value >> (size.bit_length() - 1), value & (size - 1)
    return value // size, value % size


def two_parts(value):
    high = value.astype(jnp.bfloat16).astype(jnp.float32)
    return high, value - high


def kernel(
    nx, ny, nz,
    ctrl, diff, ptile, pcell, oprof, ofield, olevel, oweight, innov, oprec,
    grad_out, dep_out,
    pack_e, pack_w, w_ext, e_ext, south_c, north_c, south_d, north_d,
    codes, field_a, field_b, rate_e, rate_w, rate_n, rate_0,
    gather_lhs, gathered, col_in, col_all, adj_part, adj_in, adj_all, spread,
    halo_send, halo_recv, code_send, code_recv, col_send, col_recv,
    lev_send, lev_recv, red_send, red_recv, adj_send, adj_recv,
):
    fields, _, cy, cx = ctrl.shape
    tiles = nx * ny
    rows = cy + 2 * HALO
    gx, gy, gz = lax.axis_index("gx"), lax.axis_index("gy"), lax.axis_index("obs")
    me = gx * ny + gy
    east, west = lax.rem(gx + 1, nx), lax.rem(gx + nx - 1, nx)
    north, south = lax.rem(gy + 1, ny), lax.rem(gy + ny - 1, ny)

    def tile_device(tile):
        return {"gx": lax.div(tile, ny), "gy": lax.rem(tile, ny), "obs": gz}

    def level_device(level):
        return {"gx": gx, "gy": gy, "obs": level}

    def other_tile(i):
        return lax.rem(me + i, tiles)

    def other_level(i):
        return lax.rem(gz + i, nz)

    barrier = pltpu.get_barrier_semaphore()

    @pl.loop(1, tiles)
    def _(i):
        pl.semaphore_signal(barrier, inc=1, device_id=tile_device(other_tile(i)), device_id_type=MESH)

    @pl.loop(1, nz)
    def _(i):
        pl.semaphore_signal(barrier, inc=1, device_id=level_device(other_level(i)), device_id_type=MESH)

    lane = lax.broadcasted_iota(jnp.int32, (cy, LANES), 1)
    first = jnp.zeros((cy, LANES), jnp.float32)
    last = jnp.zeros((cy, LANES), jnp.float32)
    for j in range(fields + 2):
        plane = ctrl[j, 0] if j < fields else diff[j - fields, 0]
        here = (lane >= HALO * j) & (lane < HALO * (j + 1))
        last = jnp.where(here, pltpu.roll(plane, (HALO * (j + 1)) % LANES, 1), last)
        moved = plane if j == 0 else pltpu.roll(plane, HALO * j, 1)
        first = jnp.where(here, moved, first)
    pack_e[...] = last
    pack_w[...] = first
    codes[me, 0:1] = ptile[...]
    codes[me, 1:2] = pcell[...]

    pl.semaphore_wait(barrier, tiles - 1 + nz - 1)

    low, high = pl.ds(0, HALO), pl.ds(cy - HALO, HALO)
    ext_low, ext_mid, ext_high = pl.ds(0, HALO), pl.ds(HALO, cy), pl.ds(HALO + cy, HALO)
    routes = (
        (pack_e, w_ext.at[ext_mid], east, gy),
        (pack_w, e_ext.at[ext_mid], west, gy),
        (ctrl.at[:, 0, high], south_c, gx, north),
        (ctrl.at[:, 0, low], north_c, gx, south),
        (diff.at[:, 0, high], south_d, gx, north),
        (diff.at[:, 0, low], north_d, gx, south),
        (pack_e.at[high], w_ext.at[ext_low], east, north),
        (pack_e.at[low], w_ext.at[ext_high], east, south),
        (pack_w.at[high], e_ext.at[ext_low], west, north),
        (pack_w.at[low], e_ext.at[ext_high], west, south),
    )
    halo_copies = [
        pltpu.make_async_remote_copy(
            src_ref=src,
            dst_ref=dst,
            send_sem=halo_send.at[n],
            recv_sem=halo_recv.at[n],
            device_id={"gx": to_x, "gy": to_y, "obs": gz},
            device_id_type=MESH,
        )
        for n, (src, dst, to_x, to_y) in enumerate(routes)
    ]
    for copy in halo_copies:
        copy.start()

    def tile_copy(src, dst, send, recv, i, source):
        return pltpu.make_async_remote_copy(
            src_ref=src,
            dst_ref=dst.at[source],
            send_sem=send.at[i],
            recv_sem=recv.at[source],
            device_id=tile_device(other_tile(i)),
            device_id_type=MESH,
        )

    def level_copy(src, dst, send, recv, i, source):
        return pltpu.make_async_remote_copy(
            src_ref=src,
            dst_ref=dst.at[source],
            send_sem=send.at[i],
            recv_sem=recv.at[source],
            device_id=level_device(other_level(i)),
            device_id_type=MESH,
        )

    @pl.loop(1, tiles)
    def _(i):
        tile_copy(codes.at[me], codes, code_send, code_recv, i, me).start()

    for copy in halo_copies:
        copy.wait()

    lane_x = lax.broadcasted_iota(jnp.int32, (rows, LANES), 1)

    def aux_plane(j):
        from_east = e_ext[...] if j == 0 else pltpu.roll(e_ext[...], LANES - HALO * j, 1)
        from_west = pltpu.roll(w_ext[...], LANES - HALO * (j + 1), 1)
        rest = jnp.where(lane_x >= LANES - HALO, from_west, 0.0)
        return jnp.where(lane_x < HALO, from_east, rest)

    def put_plane(target, s, plane):
        target[pl.ds(s, rows, stride=GROUP), :] = plane

    for f in range(fields):
        field_a[pl.ds(f, HALO, stride=GROUP), :] = south_c[f]
        field_a[pl.ds(GROUP * HALO + f, cy, stride=GROUP), :] = ctrl[f, 0]
        field_a[pl.ds(GROUP * (HALO + cy) + f, HALO, stride=GROUP), :] = north_c[f]
        put_plane(field_a, fields + f, aux_plane(f))

    lat_count = ny * cy
    row_x = lax.broadcasted_iota(jnp.int32, (rows, LANES), 0) + (gy * cy - HALO)
    wall = (row_x == lat_count - 1) | (row_x == -1)

    def main_plane(k):
        return jnp.concatenate([south_d[k], diff[k, 0], north_d[k]], axis=0)

    e_main, e_aux = main_plane(0), aux_plane(fields)
    n_main = jnp.where(wall, 0.0, main_plane(1))
    n_aux = jnp.where(wall, 0.0, aux_plane(fields + 1))
    w_main = pltpu.roll(jnp.where(lane_x == LANES - 1, e_aux, e_main), 1, 1)
    w_aux = pltpu.roll(jnp.where(lane_x == LANES - 1, e_main, e_aux), 1, 1)
    c_main = 1.0 - (e_main + w_main + n_main + pltpu.roll(n_main, 1, 0))
    c_aux = 1.0 - (e_aux + w_aux + n_aux + pltpu.roll(n_aux, 1, 0))
    for target, main, aux in (
        (rate_e, e_main, e_aux),
        (rate_w, w_main, w_aux),
        (rate_n, n_main, n_aux),
        (rate_0, c_main, c_aux),
    ):
        for f in range(fields):
            put_plane(target, f, main)
            put_plane(target, fields + f, aux)

    size = CHUNK * GROUP
    lane_c = lax.broadcasted_iota(jnp.int32, (size, LANES), 1)
    margin = HALO - STEPS - 2
    chunks = (rows - 2 * margin) // CHUNK

    def step(old, new):
        @pl.loop(0, chunks)
        def _(c):
            at = pl.multiple_of((margin + c * CHUNK) * GROUP, GROUP)
            here, before = pl.ds(at, size), pl.ds(at - GROUP, size)
            after = pl.ds(at + GROUP, size)
            v = old[here, :]
            swapped = pltpu.roll(v.reshape(CHUNK, GROUP, LANES), fields, 1).reshape(size, LANES)
            v_west = pltpu.roll(jnp.where(lane_c == LANES - 1, swapped, v), 1, 1)
            v_east = pltpu.roll(jnp.where(lane_c == 0, swapped, v), LANES - 1, 1)
            new[here, :] = (
                rate_0[here, :] * v
                + rate_e[here, :] * v_east
                + rate_w[here, :] * v_west
                + rate_n[here, :] * old[after, :]
                + rate_n[before, :] * old[before, :]
            )

    def diffuse():
        @pl.loop(0, STEPS // 2)
        def _(_):
            step(field_a, field_b)
            step(field_b, field_a)

    diffuse()

    for f in range(fields):
        turned = field_a[pl.ds(GROUP * HALO + f, cy, stride=GROUP), :].T
        big, small = two_parts(turned)
        gather_lhs[pl.ds(f * cx, cx), 0:cy] = big.astype(jnp.bfloat16)
        gather_lhs[pl.ds(f * cx, cx), cy : 2 * cy] = small.astype(jnp.bfloat16)

    profs = codes.shape[2]
    row_p = lax.broadcasted_iota(jnp.int32, (cy, profs), 0)

    def gather_for(tile):
        holder, cell = codes[tile, 0:1], codes[tile, 1:2]
        y, x = halves(cell, cx)
        y = jnp.where(holder == me, y, -1)
        pick = (row_p == y).astype(jnp.float32).astype(jnp.bfloat16)
        found = jnp.dot(
            gather_lhs[...],
            jnp.concatenate([pick, pick], axis=0),
            preferred_element_type=jnp.float32,
        )
        column = row_p == x
        sums = [
            jnp.sum(jnp.where(column, found[f * cx : (f + 1) * cx], 0.0), axis=0, keepdims=True)
            for f in range(fields)
        ]
        return jnp.concatenate(sums + [jnp.zeros((GROUP - fields, profs), jnp.float32)], axis=0)

    @pl.loop(1, tiles)
    def _(i):
        tile = other_tile(i)
        copy = tile_copy(codes.at[tile], codes, code_send, code_recv, i, tile)
        copy.wait_recv()
        gathered[i] = gather_for(tile)
        tile_copy(gathered.at[i], col_in, col_send, col_recv, i, me).start()

    col_in[me] = gather_for(me)

    total = col_in[me]
    gathered[0] = total

    @pl.loop(1, tiles)
    def _(i):
        tile = other_tile(i)
        tile_copy(gathered.at[i], col_in, col_send, col_recv, i, tile).wait_recv()
        gathered[0] = gathered[0] + col_in[tile]

    col_all[gz] = gathered[0]

    @pl.loop(1, nz)
    def _(i):
        level_copy(col_all.at[gz], col_all, lev_send, lev_recv, i, gz).start()

    obs_count = oprof.shape[1]
    match = lax.broadcasted_iota(jnp.int32, (profs, obs_count), 0) == oprof[...]
    match = match.astype(jnp.float32).astype(jnp.bfloat16)
    slot = lax.broadcasted_iota(jnp.int32, (nz * GROUP, obs_count), 0)
    wanted = olevel[...] * GROUP + ofield[...]
    weight = oweight[...]
    mix = jnp.where(slot == wanted, weight, jnp.where(slot == wanted + GROUP, 1.0 - weight, 0.0))

    @pl.loop(1, nz)
    def _(i):
        level = other_level(i)
        level_copy(col_all.at[level], col_all, lev_send, lev_recv, i, level).wait_recv()

    wide = nz * GROUP
    big, small = two_parts(col_all[...].reshape(wide, profs))
    both = jnp.concatenate([big, small], axis=0).astype(jnp.bfloat16)
    seen = jnp.dot(both, match, preferred_element_type=jnp.float32)
    seen = seen[0:wide] + seen[wide:]
    observed = jnp.sum(mix * seen, axis=0, keepdims=True)
    departures = oprec[...] * (observed - innov[...])
    dep_out[...] = departures
    big, small = two_parts(mix * departures)
    both = jnp.concatenate([big, small], axis=0).astype(jnp.bfloat16)
    back = lax.dot_general(
        both, match, (((1,), (1,)), ((), ())), preferred_element_type=jnp.float32
    )
    adj_part[...] = (back[0:wide] + back[wide:]).reshape(nz, GROUP, profs)

    @pl.loop(1, nz)
    def _(i):
        level_copy(adj_part.at[other_level(i)], adj_in, red_send, red_recv, i, gz).start()

    gathered[0] = adj_part[gz]

    @pl.loop(1, nz)
    def _(i):
        level = other_level(i)
        level_copy(adj_part.at[level], adj_in, red_send, red_recv, i, level).wait_recv()
        gathered[0] = gathered[0] + adj_in[level]

    adj_all[me] = gathered[0]

    @pl.loop(1, tiles)
    def _(i):
        tile_copy(adj_all.at[me], adj_all, adj_send, adj_recv, i, me).start()

    row_r = lax.broadcasted_iota(jnp.int32, (rows, profs), 0)
    row_c = lax.broadcasted_iota(jnp.int32, (2 * LANES, profs), 0)

    def scatter_from(tile):
        holder, cell = codes[tile, 0:1], codes[tile, 1:2]
        holder_x, holder_y = halves(holder, ny)
        y, x = halves(cell, cx)
        near = row_r == (holder_y - gy) * cy + y + HALO
        side = ((holder_x == east) & (x < cx // 2)) | ((holder_x == west) & (x >= cx // 2))
        place = jnp.where(holder_x == gx, x, jnp.where(side, LANES + x, -1))
        spots = (row_c == place).astype(jnp.float32).astype(jnp.bfloat16)
        amounts = adj_all[tile]
        big, small = two_parts(amounts)
        lines = []
        for f in range(fields):
            parts = [
                jnp.where(near, part[f : f + 1], 0.0).astype(jnp.bfloat16) for part in (big, small)
            ]
            lines.append(jnp.concatenate(parts, axis=1))
        return lax.dot_general(
            jnp.concatenate(lines, axis=0),
            jnp.concatenate([spots, spots], axis=1),
            (((1,), (1,)), ((), ())),
            preferred_element_type=jnp.float32,
        )

    spread[...] = scatter_from(me)

    @pl.loop(1, tiles)
    def _(i):
        tile = other_tile(i)
        tile_copy(adj_all.at[me], adj_all, adj_send, adj_recv, i, tile).wait_recv()
        spread[...] += scatter_from(tile)

    for f in range(fields):
        put_plane(field_a, f, spread[pl.ds(f * rows, rows), 0:LANES])
        put_plane(field_a, fields + f, spread[pl.ds(f * rows, rows), LANES : 2 * LANES])

    diffuse()

    for f in range(fields):
        grad_out[f, 0] = field_a[pl.ds(GROUP * HALO + f, cy, stride=GROUP), :]

    @pl.loop(1, tiles)
    def _(i):
        tile_copy(codes.at[me], codes, code_send, code_recv, i, me).wait_send()
        tile_copy(gathered.at[i], col_in, col_send, col_recv, i, me).wait_send()
        tile_copy(adj_all.at[me], adj_all, adj_send, adj_recv, i, me).wait_send()

    @pl.loop(1, nz)
    def _(i):
        level_copy(col_all.at[gz], col_all, lev_send, lev_recv, i, gz).wait_send()
        level_copy(adj_part.at[other_level(i)], adj_in, red_send, red_recv, i, gz).wait_send()


def per_device(
    nx, ny, nz,
    control,
    diffusivity,
    prof_tile,
    prof_cell,
    obs_prof,
    obs_field,
    obs_level,
    obs_weight,
    innovation,
    obs_precision,
):
    fields, _, cy, cx = control.shape
    profs = prof_cell.shape[0]
    obs_count = obs_prof.shape[0]
    tiles = nx * ny
    rows = cy + 2 * HALO
    f32 = jnp.float32

    def plane(*shape):
        return pltpu.VMEM(shape, f32)

    def flags(count):
        return pltpu.SemaphoreType.DMA((count,))

    scratch = [
        plane(cy, LANES), plane(cy, LANES), plane(rows, LANES), plane(rows, LANES),
        plane(fields, HALO, LANES), plane(fields, HALO, LANES),
        plane(2, HALO, LANES), plane(2, HALO, LANES),
        pltpu.VMEM((tiles, 2, profs), jnp.int32),
    ]
    scratch += [plane(rows * GROUP, LANES)] * 6
    scratch += [
        pltpu.VMEM((fields * cx, 2 * cy), jnp.bfloat16),
        plane(tiles, GROUP, profs),
        plane(tiles, GROUP, profs),
        plane(nz, GROUP, profs),
        plane(nz, GROUP, profs),
        plane(nz, GROUP, profs),
        plane(tiles, GROUP, profs),
        plane(fields * rows, 2 * LANES),
        flags(10), flags(10),
        flags(tiles), flags(tiles), flags(tiles), flags(tiles),
        flags(nz), flags(nz), flags(nz), flags(nz),
        flags(tiles), flags(tiles),
    ]
    spread, departures = pl.pallas_call(
        functools.partial(kernel, nx, ny, nz),
        out_shape=(
            jax.ShapeDtypeStruct(control.shape, f32),
            jax.ShapeDtypeStruct((1, obs_count), f32),
        ),
        in_specs=[pl.BlockSpec(memory_space=pltpu.VMEM)] * 10,
        out_specs=(pl.BlockSpec(memory_space=pltpu.VMEM),) * 2,
        scratch_shapes=scratch,
        compiler_params=pltpu.CompilerParams(
            collective_id=0, has_side_effects=True, vmem_limit_bytes=48 * 1024 * 1024
        ),
    )(
        control,
        diffusivity,
        prof_tile.reshape(1, profs),
        prof_cell.reshape(1, profs),
        obs_prof.reshape(1, obs_count),
        obs_field.reshape(1, obs_count),
        obs_level.reshape(1, obs_count),
        obs_weight.reshape(1, obs_count),
        innovation.reshape(1, obs_count),
        obs_precision.reshape(1, obs_count),
    )
    return (control + spread, departures.reshape(obs_count))


def solution(mesh):
    nx, ny, nz = mesh.shape["gx"], mesh.shape["gy"], mesh.shape["obs"]
    in_specs = (
        P(None, "obs", "gy", "gx"),
        P(None, "obs", "gy", "gx"),
        P(("gx", "gy"), None),
        P(("gx", "gy")),
        P(("gx", "gy", "obs")),
        P(("gx", "gy", "obs")),
        P(("gx", "gy", "obs")),
        P(("gx", "gy", "obs")),
        P(("gx", "gy", "obs")),
        P(("gx", "gy", "obs")),
    )
    out_specs = (P(None, "obs", "gy", "gx"), P(("gx", "gy", "obs")))
    return jax.shard_map(
        functools.partial(per_device, nx, ny, nz),
        mesh=mesh,
        in_specs=in_specs,
        out_specs=out_specs,
        check_vma=False,
    )
```

time: 399 us -> 72.7 us (0.18)
  waiting for transfers between devices: 212 us -> 0 us
  starting transfers between devices: 69.7 us -> 0 us
  Pallas kernels: 0 us -> 67.2 us
  blocking collectives: 41.3 us -> 0 us
  local copies, waits for them, and re-layouts: 39 us -> 3.83 us
  other arithmetic: 33.9 us -> 0.73 us
    ppermute x82 -> x0, waiting for transfers between devices: 204 us -> none  [the longest x40 130 us: with_halo(): lax.ppermute(lax.slice_in_dim(block, 0, width, axis=dim), axis, backward)]
    pallas_call x0 -> x1, Pallas kernels: none -> 67.2 us  [per_device(): pl.pallas_call(functools.partial(kernel, nx, ny, nz), out_shape=(jax.Shap...]
    ppermute x82 -> x0, starting transfers between devices: 57.8 us -> none  [the longest x40 27.9 us: with_halo(): lax.ppermute(lax.slice_in_dim(block, block.shape[dim] - width, None, axis...]
    all_gather x1 -> x0, blocking collectives: 22.8 us -> none  [per_device(): columns = lax.all_gather(slab, 'obs', axis=1, tiled=True)]
    unnamed x1 -> x0, blocking collectives: 18.5 us -> none
    scatter-add x3 -> x0, other arithmetic: 17.2 us -> none  [the longest x1 10.6 us: per_device(): jnp.zeros((flat_levels, lat_cells * lon_cells), jnp.float32).at[:, cells]]
    gather x5 -> x0, local copies, waits for them, and re-layouts: 13.7 us -> none  [the longest x2 6.37 us: per_device(): found = jnp.take(flat_field, asked[:, 0, :], axis=1)]
    all_to_all x3 -> x0, starting transfers between devices: 11.8 us -> none  [the longest x1 5.17 us: per_device(): lax.all_to_all(requests.reshape(holders, 1, capacity), ('gx', 'gy'), spli...]
  transfers between devices with their start and end apart: 85 -> 0, of which waited for: 82 -> 0; matrix products, arithmetic and copies ran while one was open for 5% -> 0% of each run, Pallas kernels for 0% -> 0%
where the time goes in v1:
time: 72.7 us; the launch traced here: 72.5 us
  Pallas kernels  67.2 us (92%)
  local copies, waits for them, and re-layouts  3.83 us (5%)
  other arithmetic  0.73 us (1%)
    pallas_call x1, Pallas kernels, per_device(): pl.pallas_call(functools.partial(kernel, nx, ny, nz), out_shape=(jax.Shap...  67.2 us
    unnamed x21, local copies, waits for them, and re-layouts  3.83 us

profile of v1, /device:TPU:0, one launch (start us, length us, event | category | flops | bytes accessed | tf_op | source)
XLA Modules:
  0.0 72.5 jit_solution(8069610931241480989)
XLA Ops:
  0.6 0.0 copy-start.8
  0.6 0.0 copy-start.7
  0.7 0.0 copy-start.6
  0.7 0.0 copy-start.5
  0.7 0.0 copy-start.4
  0.7 0.0 copy-start.3
  0.7 0.0 copy-start.2
  0.7 0.6 copy-done.8
  1.3 0.0 copy-done.7
  1.3 0.0 copy-done.6
  1.3 0.0 copy-done.5
  1.4 0.0 copy-done.4
  1.4 0.0 copy-done.3
  1.4 0.0 copy-done.2
  1.4 0.0 copy-start
  1.4 0.9 %copy-done = f32[4,1,128,128]{3,2,1,0:T(8,128)S(1)} copy-done((f32[4,1,128,128]{3,2,1,0:T(8,128)S(1)}, f32[4,1,128,128]{3,2,1,0:T(8,128)}, u32[]{:S(2)}) %copy-start) | copy-done | bytes 262168
  2.4 0.0 copy-start.1
  2.4 0.9 %copy-done.1 = f32[2,1,128,128]{3,2,1,0:T(8,128)S(1)} copy-done((f32[2,1,128,128]{3,2,1,0:T(8,128)S(1)}, f32[2,1,128,128]{3,2,1,0:T(8,128)}, u32[]{:S(2)}) %copy-start.1) | copy-done | bytes 131096
  3.3 0.0 copy-start.9
  3.3 0.7 copy-done.9
  3.9 67.2 %shard_map.113 = (f32[4,1,128,128]{3,2,1,0:T(8,128)S(1)}, f32[1,512]{1,0:T(1,128)S(1)}) custom-call(f32[4,1,128,128]{3,2,1,0:T(8,128)S(1)} %copy-done, f32[2,1,128,128]{3,2,1,0:T(8,128)S(1)} %copy-done.1, s32[1,512]{1,0:T(1,128)S(1)} %bitcast.9, s32[1,512]{1,0:T(1,128)S(1)} %bitcast.10, s32[1,512]{1,0:T(1,128)S(1)} %bitcast.11, s32[1,512]{1,0:T(1,128)S(1)} %bitcast.12, ...), custom_call_target="tpu_custom_call" | custom-call | tf_op jit(solution)/shard_map/pallas_call | solution.py:411
  71.2 0.7 %add.3 = f32[4,1,128,128]{3,2,1,0:T(8,128)} add(f32[4,1,128,128]{3,2,1,0:T(8,128)S(1)} %copy-done, f32[4,1,128,128]{3,2,1,0:T(8,128)S(1)} %get-tuple-element.4) | non-fusion elementwise | flops 65536 | bytes 786432 | tf_op jit(solution)/shard_map/add | solution.py:435
  71.9 0.6 copy.13
Async XLA Ops:
  0.6 0.7 copy-start.8
  0.6 0.7 copy-start.7
  0.7 0.7 copy-start.6
  0.7 0.7 copy-start.5
  0.7 0.7 copy-start.4
  0.7 0.7 copy-start.3
  0.7 0.7 copy-start.2
  1.4 0.9 %copy-start = (f32[4,1,128,128]{3,2,1,0:T(8,128)S(1)}, f32[4,1,128,128]{3,2,1,0:T(8,128)}, u32[]{:S(2)}) copy-start(f32[4,1,128,128]{3,2,1,0:T(8,128)} %ctrl.1) | copy-start | bytes 786436
  2.4 0.9 %copy-start.1 = (f32[2,1,128,128]{3,2,1,0:T(8,128)S(1)}, f32[2,1,128,128]{3,2,1,0:T(8,128)}, u32[]{:S(2)}) copy-start(f32[2,1,128,128]{3,2,1,0:T(8,128)} %diff.1) | copy-start | bytes 393220
  3.3 0.7 copy-start.9

commit v2 on v1

--- a/solution.py
+++ b/solution.py
@@ -11,7 +11,7 @@
 HALO = 16
 LANES = 128
 GROUP = 8
-CHUNK = 8
+CHUNK = 38
 MESH = pl.DeviceIdType.MESH
 
 
@@ -28,8 +28,9 @@
 
 def kernel(
     nx, ny, nz,
-    ctrl, diff, ptile, pcell, oprof, ofield, olevel, oweight, innov, oprec,
+    ctrl_in, diff_in, ptile_in, pcell_in, oprof_in, ofield_in, olevel_in, oweight_in, innov_in, oprec_in,
     grad_out, dep_out,
+    ctrl, diff, ptile, pcell, oprof, ofield, olevel, oweight, innov, oprec, fetched, match, mix,
     pack_e, pack_w, w_ext, e_ext, south_c, north_c, south_d, north_d,
     codes, field_a, field_b, rate_e, rate_w, rate_n, rate_0,
     gather_lhs, gathered, col_in, col_all, adj_part, adj_in, adj_all, spread,
@@ -56,6 +57,17 @@
     def other_level(i):
         return lax.rem(gz + i, nz)
 
+    fetches = [
+        pltpu.make_async_copy(src, dst, fetched.at[n])
+        for n, (src, dst) in enumerate((
+            (ctrl_in, ctrl), (diff_in, diff), (ptile_in, ptile), (pcell_in, pcell),
+            (oprof_in, oprof), (ofield_in, ofield), (olevel_in, olevel),
+            (oweight_in, oweight), (innov_in, innov), (oprec_in, oprec),
+        ))
+    ]
+    for fetch in fetches:
+        fetch.start()
+
     barrier = pltpu.get_barrier_semaphore()
 
     @pl.loop(1, tiles)
@@ -65,6 +77,9 @@
     @pl.loop(1, nz)
     def _(i):
         pl.semaphore_signal(barrier, inc=1, device_id=level_device(other_level(i)), device_id_type=MESH)
+
+    for fetch in fetches[0:4]:
+        fetch.wait()
 
     lane = lax.broadcasted_iota(jnp.int32, (cy, LANES), 1)
     first = jnp.zeros((cy, LANES), jnp.float32)
@@ -134,6 +149,17 @@
     def _(i):
         tile_copy(codes.at[me], codes, code_send, code_recv, i, me).start()
 
+    for fetch in fetches[4:]:
+        fetch.wait()
+
+    profs, obs_count = codes.shape[2], oprof.shape[1]
+    row_m = lax.broadcasted_iota(jnp.int32, (profs, obs_count), 0)
+    match[...] = (row_m == oprof[...]).astype(jnp.float32).astype(jnp.bfloat16)
+    slot = lax.broadcasted_iota(jnp.int32, (nz * GROUP, obs_count), 0)
+    wanted = olevel[...] * GROUP + ofield[...]
+    weight = oweight[...]
+    mix[...] = jnp.where(slot == wanted, weight, jnp.where(slot == wanted + GROUP, 1.0 - weight, 0.0))
+
     for copy in halo_copies:
         copy.wait()
 
@@ -164,16 +190,7 @@
     e_main, e_aux = main_plane(0), aux_plane(fields)
     n_main = jnp.where(wall, 0.0, main_plane(1))
     n_aux = jnp.where(wall, 0.0, aux_plane(fields + 1))
-    w_main = pltpu.roll(jnp.where(lane_x == LANES - 1, e_aux, e_main), 1, 1)
-    w_aux = pltpu.roll(jnp.where(lane_x == LANES - 1, e_main, e_aux), 1, 1)
-    c_main = 1.0 - (e_main + w_main + n_main + pltpu.roll(n_main, 1, 0))
-    c_aux = 1.0 - (e_aux + w_aux + n_aux + pltpu.roll(n_aux, 1, 0))
-    for target, main, aux in (
-        (rate_e, e_main, e_aux),
-        (rate_w, w_main, w_aux),
-        (rate_n, n_main, n_aux),
-        (rate_0, c_main, c_aux),
-    ):
+    for target, main, aux in ((rate_e, e_main, e_aux), (rate_n, n_main, n_aux)):
         for f in range(fields):
             put_plane(target, f, main)
             put_plane(target, fields + f, aux)
@@ -182,6 +199,21 @@
     lane_c = lax.broadcasted_iota(jnp.int32, (size, LANES), 1)
     margin = HALO - STEPS - 2
     chunks = (rows - 2 * margin) // CHUNK
+
+    def swap(v):
+        return pltpu.roll(v.reshape(CHUNK, GROUP, LANES), fields, 1).reshape(size, LANES)
+
+    def from_west(v, swapped):
+        return pltpu.roll(jnp.where(lane_c == LANES - 1, swapped, v), 1, 1)
+
+    @pl.loop(0, chunks)
+    def _(c):
+        at = pl.multiple_of((margin + c * CHUNK) * GROUP, GROUP)
+        here, before = pl.ds(at, size), pl.ds(at - GROUP, size)
+        e, n = rate_e[here, :], rate_n[here, :]
+        w = from_west(e, swap(e))
+        rate_w[here, :] = w
+        rate_0[here, :] = 1.0 - (e + w + n + rate_n[before, :])
 
     def step(old, new):
         @pl.loop(0, chunks)
@@ -190,8 +222,8 @@
             here, before = pl.ds(at, size), pl.ds(at - GROUP, size)
             after = pl.ds(at + GROUP, size)
             v = old[here, :]
-            swapped = pltpu.roll(v.reshape(CHUNK, GROUP, LANES), fields, 1).reshape(size, LANES)
-            v_west = pltpu.roll(jnp.where(lane_c == LANES - 1, swapped, v), 1, 1)
+            swapped = swap(v)
+            v_west = from_west(v, swapped)
             v_east = pltpu.roll(jnp.where(lane_c == 0, swapped, v), LANES - 1, 1)
             new[here, :] = (
                 rate_0[here, :] * v
@@ -215,7 +247,6 @@
         gather_lhs[pl.ds(f * cx, cx), 0:cy] = big.astype(jnp.bfloat16)
         gather_lhs[pl.ds(f * cx, cx), cy : 2 * cy] = small.astype(jnp.bfloat16)
 
-    profs = codes.shape[2]
     row_p = lax.broadcasted_iota(jnp.int32, (cy, profs), 0)
 
     def gather_for(tile):
@@ -260,14 +291,6 @@
     def _(i):
         level_copy(col_all.at[gz], col_all, lev_send, lev_recv, i, gz).start()
 
-    obs_count = oprof.shape[1]
-    match = lax.broadcasted_iota(jnp.int32, (profs, obs_count), 0) == oprof[...]
-    match = match.astype(jnp.float32).astype(jnp.bfloat16)
-    slot = lax.broadcasted_iota(jnp.int32, (nz * GROUP, obs_count), 0)
-    wanted = olevel[...] * GROUP + ofield[...]
-    weight = oweight[...]
-    mix = jnp.where(slot == wanted, weight, jnp.where(slot == wanted + GROUP, 1.0 - weight, 0.0))
-
     @pl.loop(1, nz)
     def _(i):
         level = other_level(i)
@@ -276,15 +299,15 @@
     wide = nz * GROUP
     big, small = two_parts(col_all[...].reshape(wide, profs))
     both = jnp.concatenate([big, small], axis=0).astype(jnp.bfloat16)
-    seen = jnp.dot(both, match, preferred_element_type=jnp.float32)
+    seen = jnp.dot(both, match[...], preferred_element_type=jnp.float32)
     seen = seen[0:wide] + seen[wide:]
-    observed = jnp.sum(mix * seen, axis=0, keepdims=True)
+    observed = jnp.sum(mix[...] * seen, axis=0, keepdims=True)
     departures = oprec[...] * (observed - innov[...])
     dep_out[...] = departures
-    big, small = two_parts(mix * departures)
+    big, small = two_parts(mix[...] * departures)
     both = jnp.concatenate([big, small], axis=0).astype(jnp.bfloat16)
     back = lax.dot_general(
-        both, match, (((1,), (1,)), ((), ())), preferred_element_type=jnp.float32
+        both, match[...], (((1,), (1,)), ((), ())), preferred_element_type=jnp.float32
     )
     adj_part[...] = (back[0:wide] + back[wide:]).reshape(nz, GROUP, profs)
 
@@ -387,7 +410,16 @@
     def flags(count):
         return pltpu.SemaphoreType.DMA((count,))
 
+    def numbers(count):
+        return pltpu.VMEM((1, count), jnp.int32)
+
     scratch = [
+        plane(*control.shape), plane(*diffusivity.shape), numbers(profs), numbers(profs),
+        numbers(obs_count), numbers(obs_count), numbers(obs_count),
+        plane(1, obs_count), plane(1, obs_count), plane(1, obs_count), flags(10),
+        pltpu.VMEM((profs, obs_count), jnp.bfloat16), plane(nz * GROUP, obs_count),
+    ]
+    scratch += [
         plane(cy, LANES), plane(cy, LANES), plane(rows, LANES), plane(rows, LANES),
         plane(fields, HALO, LANES), plane(fields, HALO, LANES),
         plane(2, HALO, LANES), plane(2, HALO, LANES),
@@ -414,11 +446,11 @@
             jax.ShapeDtypeStruct(control.shape, f32),
             jax.ShapeDtypeStruct((1, obs_count), f32),
         ),
-        in_specs=[pl.BlockSpec(memory_space=pltpu.VMEM)] * 10,
+        in_specs=[pl.BlockSpec(memory_space=pltpu.HBM)] * 10,
         out_specs=(pl.BlockSpec(memory_space=pltpu.VMEM),) * 2,
         scratch_shapes=scratch,
         compiler_params=pltpu.CompilerParams(
-            collective_id=0, has_side_effects=True, vmem_limit_bytes=48 * 1024 * 1024
+            collective_id=0, has_side_effects=True, vmem_limit_bytes=64 * 1024 * 1024
         ),
     )(
         control,

time: 72.7 us -> 49.8 us (0.69)
  Pallas kernels: 67.2 us -> 46.7 us
  local copies, waits for them, and re-layouts: 3.83 us -> 0.58 us
  other arithmetic: 0.73 us -> 1.76 us
    pallas_call x1, Pallas kernels: 67.2 us -> 46.7 us  [per_device(): pl.pallas_call(functools.partial(kernel, nx, ny, nz), out_shape=(jax.Shap...]
    unnamed x21 -> x3, local copies, waits for them, and re-layouts: 3.83 us -> 0.58 us
    add x1, other arithmetic: 0.73 us -> 1.76 us  [per_device(): return (control + spread, departures.reshape(obs_count))]
where the time goes in v2:
time: 49.8 us; the launch traced here: 49.7 us
  Pallas kernels  46.7 us (94%)
  other arithmetic  1.76 us (4%)
  between operations  0.65 us (1%)
  local copies, waits for them, and re-layouts  0.58 us (1%)
    pallas_call x1, Pallas kernels, per_device(): pl.pallas_call(functools.partial(kernel, nx, ny, nz), out_shape=(jax.Shap...  46.7 us
    add x1, other arithmetic, per_device(): return (control + spread, departures.reshape(obs_count))  1.76 us

profile of v2, /device:TPU:0, one launch (start us, length us, event | category | flops | bytes accessed | tf_op | source)
XLA Modules:
  0.0 49.7 jit_solution(16372686128762743081)
XLA Ops:
  0.6 46.7 %shard_map.113 = (f32[4,1,128,128]{3,2,1,0:T(8,128)}, f32[1,512]{1,0:T(1,128)}) custom-call(f32[4,1,128,128]{3,2,1,0:T(8,128)} %ctrl_in.1, f32[2,1,128,128]{3,2,1,0:T(8,128)} %diff_in.1, s32[1,512]{1,0:T(1,128)} %bitcast.9, s32[1,512]{1,0:T(1,128)} %bitcast.10, s32[1,512]{1,0:T(1,128)} %bitcast.11, s32[1,512]{1,0:T(1,128)} %bitcast.12, s32[1,512]{1,0:T(1,128)} %bitcast.13, ...), custom_call_target="tpu_custom_call" | custom-call | tf_op jit(solution)/shard_map/pallas_call | solution.py:443
  47.3 0.0 copy-start
  47.3 1.8 %add.3 = f32[4,1,128,128]{3,2,1,0:T(8,128)} add(f32[4,1,128,128]{3,2,1,0:T(8,128)} %ctrl_in.1, f32[4,1,128,128]{3,2,1,0:T(8,128)} %get-tuple-element.4) | non-fusion elementwise | flops 65536 | bytes 786432 | tf_op jit(solution)/shard_map/add | solution.py:467
  49.1 0.0 copy-done
  49.1 0.6 %copy.13 = f32[512]{0:T(512)} copy(f32[512]{0:T(512)S(1)} %bitcast.17) | data formatting | bytes 4096
Async XLA Ops:
  47.3 1.8 %copy-start = (f32[1,512]{1,0:T(1,128)S(1)}, f32[1,512]{1,0:T(1,128)}, u32[]{:S(2)}) copy-start(f32[1,512]{1,0:T(1,128)} %get-tuple-element.5) | copy-start | bytes 6148

commit v3 on v2

--- a/solution.py
+++ b/solution.py
@@ -11,7 +11,6 @@
 HALO = 16
 LANES = 128
 GROUP = 8
-CHUNK = 38
 MESH = pl.DeviceIdType.MESH
 
 
@@ -33,7 +32,7 @@
     ctrl, diff, ptile, pcell, oprof, ofield, olevel, oweight, innov, oprec, fetched, match, mix,
     pack_e, pack_w, w_ext, e_ext, south_c, north_c, south_d, north_d,
     codes, field_a, field_b, rate_e, rate_w, rate_n, rate_0,
-    gather_lhs, gathered, col_in, col_all, adj_part, adj_in, adj_all, spread,
+    gather_lhs, gathered, col_in, col_all, adj_part, adj_in, adj_all, spread, spots, nears,
     halo_send, halo_recv, code_send, code_recv, col_send, col_recv,
     lev_send, lev_recv, red_send, red_recv, adj_send, adj_recv,
 ):
@@ -155,10 +154,10 @@
     profs, obs_count = codes.shape[2], oprof.shape[1]
     row_m = lax.broadcasted_iota(jnp.int32, (profs, obs_count), 0)
     match[...] = (row_m == oprof[...]).astype(jnp.float32).astype(jnp.bfloat16)
-    slot = lax.broadcasted_iota(jnp.int32, (nz * GROUP, obs_count), 0)
-    wanted = olevel[...] * GROUP + ofield[...]
+    slot = lax.broadcasted_iota(jnp.int32, (nz * fields, obs_count), 0)
+    wanted = olevel[...] * fields + ofield[...]
     weight = oweight[...]
-    mix[...] = jnp.where(slot == wanted, weight, jnp.where(slot == wanted + GROUP, 1.0 - weight, 0.0))
+    mix[...] = jnp.where(slot == wanted, weight, jnp.where(slot == wanted + fields, 1.0 - weight, 0.0))
 
     for copy in halo_copies:
         copy.wait()
@@ -195,43 +194,35 @@
             put_plane(target, f, main)
             put_plane(target, fields + f, aux)
 
-    size = CHUNK * GROUP
+    margin = HALO - STEPS + 1
+    span = rows - 2 * margin
+    size = span * GROUP
+    here = pl.ds(margin * GROUP, size)
+    before, after = pl.ds((margin - 1) * GROUP, size), pl.ds((margin + 1) * GROUP, size)
     lane_c = lax.broadcasted_iota(jnp.int32, (size, LANES), 1)
-    margin = HALO - STEPS - 2
-    chunks = (rows - 2 * margin) // CHUNK
 
     def swap(v):
-        return pltpu.roll(v.reshape(CHUNK, GROUP, LANES), fields, 1).reshape(size, LANES)
-
-    def from_west(v, swapped):
+        return pltpu.roll(v.reshape(span, GROUP, LANES), fields, 1).reshape(size, LANES)
+
+    def west_of(v, swapped):
         return pltpu.roll(jnp.where(lane_c == LANES - 1, swapped, v), 1, 1)
 
-    @pl.loop(0, chunks)
-    def _(c):
-        at = pl.multiple_of((margin + c * CHUNK) * GROUP, GROUP)
-        here, before = pl.ds(at, size), pl.ds(at - GROUP, size)
-        e, n = rate_e[here, :], rate_n[here, :]
-        w = from_west(e, swap(e))
-        rate_w[here, :] = w
-        rate_0[here, :] = 1.0 - (e + w + n + rate_n[before, :])
+    e, n = rate_e[here, :], rate_n[here, :]
+    w = west_of(e, swap(e))
+    rate_w[here, :] = w
+    rate_0[here, :] = 1.0 - (e + w + n + rate_n[before, :])
 
     def step(old, new):
-        @pl.loop(0, chunks)
-        def _(c):
-            at = pl.multiple_of((margin + c * CHUNK) * GROUP, GROUP)
-            here, before = pl.ds(at, size), pl.ds(at - GROUP, size)
-            after = pl.ds(at + GROUP, size)
-            v = old[here, :]
-            swapped = swap(v)
-            v_west = from_west(v, swapped)
-            v_east = pltpu.roll(jnp.where(lane_c == 0, swapped, v), LANES - 1, 1)
-            new[here, :] = (
-                rate_0[here, :] * v
-                + rate_e[here, :] * v_east
-                + rate_w[here, :] * v_west
-                + rate_n[here, :] * old[after, :]
-                + rate_n[before, :] * old[before, :]
-            )
+        v = old[here, :]
+        swapped = swap(v)
+        v_east = pltpu.roll(jnp.where(lane_c == 0, swapped, v), LANES - 1, 1)
+        new[here, :] = (
+            rate_0[here, :] * v
+            + rate_e[here, :] * v_east
+            + rate_w[here, :] * west_of(v, swapped)
+            + rate_n[here, :] * old[after, :]
+            + rate_n[before, :] * old[before, :]
+        )
 
     def diffuse():
         @pl.loop(0, STEPS // 2)
@@ -264,7 +255,7 @@
             jnp.sum(jnp.where(column, found[f * cx : (f + 1) * cx], 0.0), axis=0, keepdims=True)
             for f in range(fields)
         ]
-        return jnp.concatenate(sums + [jnp.zeros((GROUP - fields, profs), jnp.float32)], axis=0)
+        return jnp.concatenate(sums, axis=0)
 
     @pl.loop(1, tiles)
     def _(i):
@@ -291,12 +282,24 @@
     def _(i):
         level_copy(col_all.at[gz], col_all, lev_send, lev_recv, i, gz).start()
 
+    row_r = lax.broadcasted_iota(jnp.int32, (rows, profs), 0)
+    row_c = lax.broadcasted_iota(jnp.int32, (2 * LANES, profs), 0)
+
+    @pl.loop(0, tiles)
+    def _(tile):
+        holder, cell = codes[tile, 0:1], codes[tile, 1:2]
+        holder_x, _ = halves(holder, ny)
+        _, x = halves(cell, cx)
+        side = ((holder_x == east) & (x < cx // 2)) | ((holder_x == west) & (x >= cx // 2))
+        place = jnp.where(holder_x == gx, x, jnp.where(side, LANES + x, -1))
+        spots[tile] = (row_c == place).astype(jnp.float32).astype(jnp.bfloat16)
+
     @pl.loop(1, nz)
     def _(i):
         level = other_level(i)
         level_copy(col_all.at[level], col_all, lev_send, lev_recv, i, level).wait_recv()
 
-    wide = nz * GROUP
+    wide = nz * fields
     big, small = two_parts(col_all[...].reshape(wide, profs))
     both = jnp.concatenate([big, small], axis=0).astype(jnp.bfloat16)
     seen = jnp.dot(both, match[...], preferred_element_type=jnp.float32)
@@ -309,11 +312,19 @@
     back = lax.dot_general(
         both, match[...], (((1,), (1,)), ((), ())), preferred_element_type=jnp.float32
     )
-    adj_part[...] = (back[0:wide] + back[wide:]).reshape(nz, GROUP, profs)
+    adj_part[...] = (back[0:wide] + back[wide:]).reshape(nz, fields, profs)
 
     @pl.loop(1, nz)
     def _(i):
         level_copy(adj_part.at[other_level(i)], adj_in, red_send, red_recv, i, gz).start()
+
+    @pl.loop(0, tiles)
+    def _(tile):
+        holder, cell = codes[tile, 0:1], codes[tile, 1:2]
+        _, holder_y = halves(holder, ny)
+        y, _ = halves(cell, cx)
+        near = row_r == (holder_y - gy) * cy + y + HALO
+        nears[tile] = near.astype(jnp.float32).astype(jnp.bfloat16)
 
     gathered[0] = adj_part[gz]
 
@@ -329,28 +340,17 @@
     def _(i):
         tile_copy(adj_all.at[me], adj_all, adj_send, adj_recv, i, me).start()
 
-    row_r = lax.broadcasted_iota(jnp.int32, (rows, profs), 0)
-    row_c = lax.broadcasted_iota(jnp.int32, (2 * LANES, profs), 0)
-
     def scatter_from(tile):
-        holder, cell = codes[tile, 0:1], codes[tile, 1:2]
-        holder_x, holder_y = halves(holder, ny)
-        y, x = halves(cell, cx)
-        near = row_r == (holder_y - gy) * cy + y + HALO
-        side = ((holder_x == east) & (x < cx // 2)) | ((holder_x == west) & (x >= cx // 2))
-        place = jnp.where(holder_x == gx, x, jnp.where(side, LANES + x, -1))
-        spots = (row_c == place).astype(jnp.float32).astype(jnp.bfloat16)
-        amounts = adj_all[tile]
-        big, small = two_parts(amounts)
-        lines = []
-        for f in range(fields):
-            parts = [
-                jnp.where(near, part[f : f + 1], 0.0).astype(jnp.bfloat16) for part in (big, small)
-            ]
-            lines.append(jnp.concatenate(parts, axis=1))
+        big, small = (part.astype(jnp.bfloat16) for part in two_parts(adj_all[tile]))
+        near = nears[tile]
+        lines = [
+            jnp.concatenate([near * big[f : f + 1], near * small[f : f + 1]], axis=1)
+            for f in range(fields)
+        ]
+        spot = spots[tile]
         return lax.dot_general(
             jnp.concatenate(lines, axis=0),
-            jnp.concatenate([spots, spots], axis=1),
+            jnp.concatenate([spot, spot], axis=1),
             (((1,), (1,)), ((), ())),
             preferred_element_type=jnp.float32,
         )
@@ -417,7 +417,7 @@
         plane(*control.shape), plane(*diffusivity.shape), numbers(profs), numbers(profs),
         numbers(obs_count), numbers(obs_count), numbers(obs_count),
         plane(1, obs_count), plane(1, obs_count), plane(1, obs_count), flags(10),
-        pltpu.VMEM((profs, obs_count), jnp.bfloat16), plane(nz * GROUP, obs_count),
+        pltpu.VMEM((profs, obs_count), jnp.bfloat16), plane(nz * fields, obs_count),
     ]
     scratch += [
         plane(cy, LANES), plane(cy, LANES), plane(rows, LANES), plane(rows, LANES),
@@ -428,13 +428,15 @@
     scratch += [plane(rows * GROUP, LANES)] * 6
     scratch += [
         pltpu.VMEM((fields * cx, 2 * cy), jnp.bfloat16),
-        plane(tiles, GROUP, profs),
-        plane(tiles, GROUP, profs),
-        plane(nz, GROUP, profs),
-        plane(nz, GROUP, profs),
-        plane(nz, GROUP, profs),
-        plane(tiles, GROUP, profs),
+        plane(tiles, fields, profs),
+        plane(tiles, fields, profs),
+        plane(nz, fields, profs),
+        plane(nz, fields, profs),
+        plane(nz, fields, profs),
+        plane(tiles, fields, profs),
         plane(fields * rows, 2 * LANES),
+        pltpu.VMEM((tiles, 2 * LANES, profs), jnp.bfloat16),
+        pltpu.VMEM((tiles, rows, profs), jnp.bfloat16),
         flags(10), flags(10),
         flags(tiles), flags(tiles), flags(tiles), flags(tiles),
         flags(nz), flags(nz), flags(nz), flags(nz),

time: 49.8 us -> 44.4 us (0.89)
  Pallas kernels: 46.7 us -> 41.2 us
    pallas_call x1, Pallas kernels: 46.7 us -> 41.2 us  [per_device(): pl.pallas_call(functools.partial(kernel, nx, ny, nz), out_shape=(jax.Shap...]
where the time goes in v3:
time: 44.4 us; the launch traced here: 44.2 us
  Pallas kernels  41.2 us (93%)
  other arithmetic  1.76 us (4%)
  between operations  0.65 us (1%)
  local copies, waits for them, and re-layouts  0.58 us (1%)
    pallas_call x1, Pallas kernels, per_device(): pl.pallas_call(functools.partial(kernel, nx, ny, nz), out_shape=(jax.Shap...  41.2 us
    add x1, other arithmetic, per_device(): return (control + spread, departures.reshape(obs_count))  1.76 us

profile of v3, /device:TPU:0, one launch (start us, length us, event | category | flops | bytes accessed | tf_op | source)
XLA Modules:
  0.0 44.2 jit_solution(3753902650732606793)
XLA Ops:
  0.6 41.2 %shard_map.113 = (f32[4,1,128,128]{3,2,1,0:T(8,128)}, f32[1,512]{1,0:T(1,128)}) custom-call(f32[4,1,128,128]{3,2,1,0:T(8,128)} %ctrl_in.1, f32[2,1,128,128]{3,2,1,0:T(8,128)} %diff_in.1, s32[1,512]{1,0:T(1,128)} %bitcast.9, s32[1,512]{1,0:T(1,128)} %bitcast.10, s32[1,512]{1,0:T(1,128)} %bitcast.11, s32[1,512]{1,0:T(1,128)} %bitcast.12, s32[1,512]{1,0:T(1,128)} %bitcast.13, ...), custom_call_target="tpu_custom_call" | custom-call | tf_op jit(solution)/shard_map/pallas_call | solution.py:445
  41.9 0.0 copy-start
  41.9 1.8 %add.3 = f32[4,1,128,128]{3,2,1,0:T(8,128)} add(f32[4,1,128,128]{3,2,1,0:T(8,128)} %ctrl_in.1, f32[4,1,128,128]{3,2,1,0:T(8,128)} %get-tuple-element.4) | non-fusion elementwise | flops 65536 | bytes 786432 | tf_op jit(solution)/shard_map/add | solution.py:469
  43.6 0.0 copy-done
  43.6 0.6 %copy.13 = f32[512]{0:T(512)} copy(f32[512]{0:T(512)S(1)} %bitcast.17) | data formatting | bytes 4096
Async XLA Ops:
  41.9 1.8 %copy-start = (f32[1,512]{1,0:T(1,128)S(1)}, f32[1,512]{1,0:T(1,128)}, u32[]{:S(2)}) copy-start(f32[1,512]{1,0:T(1,128)} %get-tuple-element.5) | copy-start | bytes 6148

commit v4 on v3

--- a/solution.py
+++ b/solution.py
@@ -11,6 +11,7 @@
 HALO = 16
 LANES = 128
 GROUP = 8
+BLOCK = 15
 MESH = pl.DeviceIdType.MESH
 
 
@@ -159,6 +160,17 @@
     weight = oweight[...]
     mix[...] = jnp.where(slot == wanted, weight, jnp.where(slot == wanted + fields, 1.0 - weight, 0.0))
 
+    def put_plane(target, s, plane, start=0):
+        target[pl.ds(GROUP * start + s, plane.shape[0], stride=GROUP), :] = plane
+
+    lat_count = ny * cy
+    row_y = lax.broadcasted_iota(jnp.int32, (cy, LANES), 0) + gy * cy
+    n_own = jnp.where(row_y == lat_count - 1, 0.0, diff[1, 0])
+    for f in range(fields):
+        put_plane(field_a, f, ctrl[f, 0], HALO)
+        put_plane(rate_e, f, diff[0, 0], HALO)
+        put_plane(rate_n, f, n_own, HALO)
+
     for copy in halo_copies:
         copy.wait()
 
@@ -170,59 +182,62 @@
         rest = jnp.where(lane_x >= LANES - HALO, from_west, 0.0)
         return jnp.where(lane_x < HALO, from_east, rest)
 
-    def put_plane(target, s, plane):
-        target[pl.ds(s, rows, stride=GROUP), :] = plane
-
-    for f in range(fields):
-        field_a[pl.ds(f, HALO, stride=GROUP), :] = south_c[f]
-        field_a[pl.ds(GROUP * HALO + f, cy, stride=GROUP), :] = ctrl[f, 0]
-        field_a[pl.ds(GROUP * (HALO + cy) + f, HALO, stride=GROUP), :] = north_c[f]
-        put_plane(field_a, fields + f, aux_plane(f))
-
-    lat_count = ny * cy
     row_x = lax.broadcasted_iota(jnp.int32, (rows, LANES), 0) + (gy * cy - HALO)
     wall = (row_x == lat_count - 1) | (row_x == -1)
-
-    def main_plane(k):
-        return jnp.concatenate([south_d[k], diff[k, 0], north_d[k]], axis=0)
-
-    e_main, e_aux = main_plane(0), aux_plane(fields)
-    n_main = jnp.where(wall, 0.0, main_plane(1))
+    row_s = lax.broadcasted_iota(jnp.int32, (HALO, LANES), 0) + (gy * cy - HALO)
+    e_aux = aux_plane(fields)
     n_aux = jnp.where(wall, 0.0, aux_plane(fields + 1))
-    for target, main, aux in ((rate_e, e_main, e_aux), (rate_n, n_main, n_aux)):
-        for f in range(fields):
-            put_plane(target, f, main)
-            put_plane(target, fields + f, aux)
+    n_south = jnp.where(row_s == -1, 0.0, south_d[1])
+    for f in range(fields):
+        put_plane(field_a, f, south_c[f])
+        put_plane(field_a, f, north_c[f], HALO + cy)
+        put_plane(field_a, fields + f, aux_plane(f))
+        put_plane(rate_e, f, south_d[0])
+        put_plane(rate_e, f, north_d[0], HALO + cy)
+        put_plane(rate_e, fields + f, e_aux)
+        put_plane(rate_n, f, n_south)
+        put_plane(rate_n, f, north_d[1], HALO + cy)
+        put_plane(rate_n, fields + f, n_aux)
 
     margin = HALO - STEPS + 1
     span = rows - 2 * margin
-    size = span * GROUP
-    here = pl.ds(margin * GROUP, size)
-    before, after = pl.ds((margin - 1) * GROUP, size), pl.ds((margin + 1) * GROUP, size)
-    lane_c = lax.broadcasted_iota(jnp.int32, (size, LANES), 1)
+    count = -(-span // BLOCK)
+    edges = [margin + span * k // count for k in range(count + 1)]
 
     def swap(v):
-        return pltpu.roll(v.reshape(span, GROUP, LANES), fields, 1).reshape(size, LANES)
+        return pltpu.roll(v.reshape(-1, GROUP, LANES), fields, 1).reshape(v.shape)
+
+    def lanes_of(v):
+        return lax.broadcasted_iota(jnp.int32, v.shape, 1)
 
     def west_of(v, swapped):
-        return pltpu.roll(jnp.where(lane_c == LANES - 1, swapped, v), 1, 1)
-
-    e, n = rate_e[here, :], rate_n[here, :]
-    w = west_of(e, swap(e))
-    rate_w[here, :] = w
-    rate_0[here, :] = 1.0 - (e + w + n + rate_n[before, :])
+        return pltpu.roll(jnp.where(lanes_of(v) == LANES - 1, swapped, v), 1, 1)
+
+    for low_row, high_row in zip(edges[:-1], edges[1:]):
+        size = (high_row - low_row) * GROUP
+        here = pl.ds(low_row * GROUP, size)
+        e = rate_e[here, :]
+        n = rate_n[pl.ds((low_row - 1) * GROUP, size + GROUP), :]
+        w = west_of(e, swap(e))
+        rate_w[here, :] = w
+        rate_0[here, :] = 1.0 - (e + w + n[GROUP:] + n[:-GROUP])
 
     def step(old, new):
-        v = old[here, :]
-        swapped = swap(v)
-        v_east = pltpu.roll(jnp.where(lane_c == 0, swapped, v), LANES - 1, 1)
-        new[here, :] = (
-            rate_0[here, :] * v
-            + rate_e[here, :] * v_east
-            + rate_w[here, :] * west_of(v, swapped)
-            + rate_n[here, :] * old[after, :]
-            + rate_n[before, :] * old[before, :]
-        )
+        for low_row, high_row in zip(edges[:-1], edges[1:]):
+            size = (high_row - low_row) * GROUP
+            here = pl.ds(low_row * GROUP, size)
+            n = rate_n[pl.ds((low_row - 1) * GROUP, size + GROUP), :]
+            tall = old[pl.ds((low_row - 1) * GROUP, size + 2 * GROUP), :]
+            v = tall[GROUP:-GROUP]
+            swapped = swap(v)
+            v_east = pltpu.roll(jnp.where(lanes_of(v) == 0, swapped, v), LANES - 1, 1)
+            new[here, :] = (
+                rate_0[here, :] * v
+                + rate_e[here, :] * v_east
+                + rate_w[here, :] * west_of(v, swapped)
+                + n[GROUP:] * tall[2 * GROUP :]
+                + n[:-GROUP] * tall[: -2 * GROUP]
+            )
 
     def diffuse():
         @pl.loop(0, STEPS // 2)
@@ -260,15 +275,21 @@
     @pl.loop(1, tiles)
     def _(i):
         tile = other_tile(i)
-        copy = tile_copy(codes.at[tile], codes, code_send, code_recv, i, tile)
-        copy.wait_recv()
-        gathered[i] = gather_for(tile)
-        tile_copy(gathered.at[i], col_in, col_send, col_recv, i, me).start()
-
-    col_in[me] = gather_for(me)
-
-    total = col_in[me]
-    gathered[0] = total
+        tile_copy(codes.at[tile], codes, code_send, code_recv, i, tile).wait_recv()
+
+    together = 4 if tiles % 4 == 0 else 1
+
+    @pl.loop(0, tiles // together)
+    def _(g):
+        for k in range(together):
+            i = lax.rem(g * together + k + 1, tiles)
+            gathered[i] = gather_for(other_tile(i))
+        for k in range(together):
+            i = g * together + k + 1
+
+            @pl.when(i < tiles)
+            def _():
+                tile_copy(gathered.at[i], col_in, col_send, col_recv, i, me).start()
 
     @pl.loop(1, tiles)
     def _(i):
@@ -340,28 +361,33 @@
     def _(i):
         tile_copy(adj_all.at[me], adj_all, adj_send, adj_recv, i, me).start()
 
-    def scatter_from(tile):
-        big, small = (part.astype(jnp.bfloat16) for part in two_parts(adj_all[tile]))
-        near = nears[tile]
-        lines = [
-            jnp.concatenate([near * big[f : f + 1], near * small[f : f + 1]], axis=1)
-            for f in range(fields)
-        ]
-        spot = spots[tile]
+    def scatter_from(some):
+        lines = [[] for _ in range(fields)]
+        places = []
+        for tile in some:
+            near = nears[tile]
+            for part in two_parts(adj_all[tile]):
+                part = part.astype(jnp.bfloat16)
+                places.append(spots[tile])
+                for f in range(fields):
+                    lines[f].append(near * part[f : f + 1])
         return lax.dot_general(
-            jnp.concatenate(lines, axis=0),
-            jnp.concatenate([spot, spot], axis=1),
+            jnp.concatenate([jnp.concatenate(line, axis=1) for line in lines], axis=0),
+            jnp.concatenate(places, axis=1),
             (((1,), (1,)), ((), ())),
             preferred_element_type=jnp.float32,
         )
 
-    spread[...] = scatter_from(me)
-
-    @pl.loop(1, tiles)
-    def _(i):
-        tile = other_tile(i)
-        tile_copy(adj_all.at[me], adj_all, adj_send, adj_recv, i, tile).wait_recv()
-        spread[...] += scatter_from(tile)
+    spread[...] = scatter_from([me])
+    joined = 7 if (tiles - 1) % 7 == 0 else 1
+
+    @pl.loop(0, (tiles - 1) // joined)
+    def _(g):
+        some = [other_tile(g * joined + k + 1) for k in range(joined)]
+        for k, tile in enumerate(some):
+            i = g * joined + k + 1
+            tile_copy(adj_all.at[me], adj_all, adj_send, adj_recv, i, tile).wait_recv()
+        spread[...] += scatter_from(some)
 
     for f in range(fields):
         put_plane(field_a, f, spread[pl.ds(f * rows, rows), 0:LANES])

time: 44.4 us -> 41.2 us (0.928)
  Pallas kernels: 41.2 us -> 38.1 us
    pallas_call x1, Pallas kernels: 41.2 us -> 38.1 us  [per_device(): pl.pallas_call(functools.partial(kernel, nx, ny, nz), out_shape=(jax.Shap...]
where the time goes in v4:
time: 41.2 us; the launch traced here: 41.1 us
  Pallas kernels  38.1 us (92%)
  other arithmetic  1.76 us (4%)
  between operations  0.65 us (2%)
  local copies, waits for them, and re-layouts  0.58 us (1%)
    pallas_call x1, Pallas kernels, per_device(): pl.pallas_call(functools.partial(kernel, nx, ny, nz), out_shape=(jax.Shap...  38.1 us
    add x1, other arithmetic, per_device(): return (control + spread, departures.reshape(obs_count))  1.76 us

profile of v4, /device:TPU:0, one launch (start us, length us, event | category | flops | bytes accessed | tf_op | source)
XLA Modules:
  0.0 41.1 jit_solution(2600320364580804900)
XLA Ops:
  0.6 38.1 %shard_map.113 = (f32[4,1,128,128]{3,2,1,0:T(8,128)}, f32[1,512]{1,0:T(1,128)}) custom-call(f32[4,1,128,128]{3,2,1,0:T(8,128)} %ctrl_in.1, f32[2,1,128,128]{3,2,1,0:T(8,128)} %diff_in.1, s32[1,512]{1,0:T(1,128)} %bitcast.9, s32[1,512]{1,0:T(1,128)} %bitcast.10, s32[1,512]{1,0:T(1,128)} %bitcast.11, s32[1,512]{1,0:T(1,128)} %bitcast.12, s32[1,512]{1,0:T(1,128)} %bitcast.13, ...), custom_call_target="tpu_custom_call" | custom-call | tf_op jit(solution)/shard_map/pallas_call | solution.py:471
  38.7 0.0 copy-start
  38.7 1.8 %add.3 = f32[4,1,128,128]{3,2,1,0:T(8,128)} add(f32[4,1,128,128]{3,2,1,0:T(8,128)} %ctrl_in.1, f32[4,1,128,128]{3,2,1,0:T(8,128)} %get-tuple-element.4) | non-fusion elementwise | flops 65536 | bytes 786432 | tf_op jit(solution)/shard_map/add | solution.py:495
  40.5 0.0 copy-done
  40.5 0.6 %copy.13 = f32[512]{0:T(512)} copy(f32[512]{0:T(512)S(1)} %bitcast.17) | data formatting | bytes 4096
Async XLA Ops:
  38.7 1.8 %copy-start = (f32[1,512]{1,0:T(1,128)S(1)}, f32[1,512]{1,0:T(1,128)}, u32[]{:S(2)}) copy-start(f32[1,512]{1,0:T(1,128)} %get-tuple-element.5) | copy-start | bytes 6148

commit v5 on v4

--- a/solution.py
+++ b/solution.py
@@ -478,7 +478,7 @@
         out_specs=(pl.BlockSpec(memory_space=pltpu.VMEM),) * 2,
         scratch_shapes=scratch,
         compiler_params=pltpu.CompilerParams(
-            collective_id=0, has_side_effects=True, vmem_limit_bytes=64 * 1024 * 1024
+            collective_id=0, has_side_effects=True, vmem_limit_bytes=(64 * 1024 - 750) * 1024
         ),
     )(
         control,

time: 41.2 us -> 41.2 us (level)
  no operation moved by 1% of the time
where the time goes in v5:
time: 41.2 us; the launch traced here: 41 us
  Pallas kernels  38.1 us (92%)
  other arithmetic  1.69 us (4%)
  between operations  0.67 us (2%)
  local copies, waits for them, and re-layouts  0.59 us (1%)
    pallas_call x1, Pallas kernels, per_device(): pl.pallas_call(functools.partial(kernel, nx, ny, nz), out_shape=(jax.Shap...  38.1 us
    add x1, other arithmetic, per_device(): return (control + spread, departures.reshape(obs_count))  1.69 us

profile of v5, /device:TPU:0, one launch (start us, length us, event | category | flops | bytes accessed | tf_op | source)
XLA Modules:
  0.0 41.0 jit_solution(9340334209934597723)
XLA Ops:
  0.6 0.0 copy-start
  0.6 38.1 %shard_map.113 = (f32[4,1,128,128]{3,2,1,0:T(8,128)}, f32[1,512]{1,0:T(1,128)}) custom-call(f32[4,1,128,128]{3,2,1,0:T(8,128)} %ctrl_in.1, f32[2,1,128,128]{3,2,1,0:T(8,128)} %diff_in.1, s32[1,512]{1,0:T(1,128)} %bitcast.9, s32[1,512]{1,0:T(1,128)} %bitcast.10, s32[1,512]{1,0:T(1,128)} %bitcast.11, s32[1,512]{1,0:T(1,128)} %bitcast.12, s32[1,512]{1,0:T(1,128)} %bitcast.13, ...), custom_call_target="tpu_custom_call" | custom-call | tf_op jit(solution)/shard_map/pallas_call | solution.py:471
  38.7 0.0 copy-done
  38.7 0.0 copy-start.1
  38.8 1.7 %add.3 = f32[4,1,128,128]{3,2,1,0:T(8,128)} add(f32[4,1,128,128]{3,2,1,0:T(8,128)S(1)} %copy-done, f32[4,1,128,128]{3,2,1,0:T(8,128)} %get-tuple-element.4) | non-fusion elementwise | flops 65536 | bytes 786432 | tf_op jit(solution)/shard_map/add | solution.py:495
  40.4 0.0 copy-done.1
  40.4 0.6 %copy.13 = f32[512]{0:T(512)} copy(f32[512]{0:T(512)S(1)} %bitcast.17) | data formatting | bytes 4096
Async XLA Ops:
  0.6 38.1 %copy-start = (f32[4,1,128,128]{3,2,1,0:T(8,128)S(1)}, f32[4,1,128,128]{3,2,1,0:T(8,128)}, u32[]{:S(2)}) copy-start(f32[4,1,128,128]{3,2,1,0:T(8,128)} %ctrl_in.1) | copy-start | bytes 786436
  38.7 1.7 %copy-start.1 = (f32[1,512]{1,0:T(1,128)S(1)}, f32[1,512]{1,0:T(1,128)}, u32[]{:S(2)}) copy-start(f32[1,512]{1,0:T(1,128)} %get-tuple-element.5) | copy-start | bytes 6148
